TPU v7x, 256 devices: a whole 4x4x8 slice. The times are simulated.
256 devices in a mesh: wide: 16 (over z_hi, y, core), tp: 4 (over z_lo), prompt: 4 (over x).
Axes of the slice: x: 4, y: 4, z: 8 (z_hi: 2, z_lo: 4; z = z_hi * 4 + z_lo), core: 2. Of those that a mesh axis runs over, the one named last changes fastest.
Arguments:
- span_query: bfloat16 [32768, 16, 128], P(('prompt', 'wide'), 'tp'), parts along dimension 0, may hold values from -6 to 6
- span_key: bfloat16 [32768, 16, 128], P(('prompt', 'wide'), 'tp'), parts along dimension 0, may hold values from -6 to 6
- span_value: bfloat16 [32768, 32, 128], P(('prompt', 'wide'), 'tp'), parts along dimension 0, may hold values from -6 to 6
- span_beta_logit: float32 [32768, 32], P(('prompt', 'wide'), 'tp'), parts along dimension 0, may hold values from -5 to -2
- span_logdecay: float32 [32768, 32], P(('prompt', 'wide'), 'tp'), parts along dimension 0, may hold values from -0.8 to 0
- span_gate: bfloat16 [32768, 32, 128], P(('prompt', 'wide'), 'tp'), parts along dimension 0, may hold values from -6 to 6
- norm_gain: float32 [128], replicated, may hold values from 0.1 to 1.9
- prior_state: float32 [128, 128, 128], P(('prompt', 'tp')), parts along dimension 0, may hold values from -1.25 to 1.25
- step_query: bfloat16 [64, 4, 16, 128], P(('prompt', 'wide'), None, 'tp'), parts along dimension 0, may hold values from -6 to 6
- step_key: bfloat16 [64, 4, 16, 128], P(('prompt', 'wide'), None, 'tp'), parts along dimension 0, may hold values from -6 to 6
- step_value: bfloat16 [64, 4, 32, 128], P(('prompt', 'wide'), None, 'tp'), parts along dimension 0, may hold values from -6 to 6
- step_beta_logit: float32 [64, 4, 32], P(('prompt', 'wide'), None, 'tp'), parts along dimension 0, may hold values from -2 to 1
- step_logdecay: float32 [64, 4, 32], P(('prompt', 'wide'), None, 'tp'), parts along dimension 0, may hold values from -0.7 to -0.02
- step_gate: bfloat16 [64, 4, 32, 128], P(('prompt', 'wide'), None, 'tp'), parts along dimension 0, may hold values from -6 to 6
- cache_key: bfloat16 [131072, 2, 256], P(('prompt', 'wide')), parts along dimension 0, may hold values from -6 to 6
- cache_value: bfloat16 [131072, 2, 256], P(('prompt', 'wide')), parts along dimension 0, may hold values from -6 to 6
- att_query: bfloat16 [64, 4, 16, 256], P(('prompt', 'wide'), None, 'tp'), parts along dimension 0, may hold values from -6 to 6
- att_key: bfloat16 [64, 4, 2, 256], P(('prompt', 'wide')), parts along dimension 0, may hold values from -6 to 6
- att_value: bfloat16 [64, 4, 2, 256], P(('prompt', 'wide')), parts along dimension 0, may hold values from -6 to 6
- att_gate: bfloat16 [64, 4, 16, 256], P(('prompt', 'wide'), None, 'tp'), parts along dimension 0, may hold values from -6 to 6
Outputs:
- span_out: bfloat16 [32768, 4096], P(('prompt', 'wide'), 'tp'), parts along dimension 0
- step_out: bfloat16 [64, 4, 4096], P(('prompt', 'wide'), None, 'tp'), parts along dimension 0
- final_state: float32 [64, 32, 128, 128], P(('prompt', 'wide'), 'tp'), parts along dimension 0
- att_out: bfloat16 [64, 4, 4096], P(('prompt', 'wide'), None, 'tp'), parts along dimension 0
There are 4 independent parts, one for each index of `prompt`. A program takes and returns all parts, laid end to end along the dimension named above; an argument that names none is the same for every part. Nothing has to cross between parts.
All inputs are finite; a program needn't handle non-finite values.
Results may differ from a plain program's by a relative error of at most 0.0044.
Values may be sent and summed in bfloat16 or wider, within the bound.
A program may use at most 128 MiB of HBM per device.

v0:
```python
import jax
import jax.numpy as jnp
from jax import lax
from jax.sharding import PartitionSpec as P

DK = 128
QH = 16
KVH = 2
HD = 256
STEPS = 4


peak_value = lax.Precision.HIGHEST


def prefix(part, axis, combine, identity):
    place = lax.axis_index(axis)
    gathered = jax.tree.map(lambda a: lax.all_gather(a, axis), part)
    state = jax.tree.map(lambda a, e: jnp.zeros_like(a) + jnp.asarray(e, a.dtype), part, identity)

    def one(lap, state):
        return combine(
            state, jax.tree.map(lambda a: lax.dynamic_index_in_dim(a, lap, 0, False), gathered)
        )

    return lax.fori_loop(0, place, one, state)


def broadcast(array, axis, root):
    mine = lax.axis_index(axis) == root
    return lax.psum(jnp.where(mine, array, jnp.zeros_like(array)), axis)


def unit_rows(values):
    values = values.astype(jnp.float32)
    return values / jnp.sqrt(jnp.sum(values * values, axis=-1, keepdims=True) + 1e-06)


def gated_norm(layer_output, gating, norm_gain):
    scaling = 1.0 / jnp.sqrt(jnp.mean(layer_output * layer_output, axis=-1, keepdims=True) + 1e-06)
    gating = gating.astype(jnp.float32)
    return layer_output * scaling * norm_gain * (gating * jax.nn.sigmoid(gating))


def delta_step(recurrent_state, query_vectors, key_matrix_rows, values, write_rate, retention):
    recalled_values = jnp.einsum(
        "...ow,...owy->...oy", key_matrix_rows, recurrent_state, precision=peak_value
    )
    written = (write_rate[..., None] * key_matrix_rows)[..., :, None]
    erased = recurrent_state - written * recalled_values[..., None, :]
    recurrent_state = retention[..., None, None] * erased + written * values[..., None, :]
    layer_output = jnp.einsum(
        "...ow,...owy->...oy", query_vectors, recurrent_state, precision=peak_value
    )
    return (recurrent_state, layer_output)


def block_transition(query_vectors, key_matrix_rows, values, write_rate, logdecay):
    length = key_matrix_rows.shape[1]
    value_width = values.shape[2]
    cumulative = jnp.cumsum(logdecay, axis=1)
    row_ids = lax.broadcasted_iota(jnp.int32, (length, length), 0)
    col_ids = lax.broadcasted_iota(jnp.int32, (length, length), 1)
    strictly = row_ids > col_ids
    within = row_ids >= col_ids
    spread = cumulative[:, :, None] - cumulative[:, None, :]
    ratios = jnp.exp(jnp.where(within[None], spread, -jnp.inf))
    products = jnp.einsum("hck,hik->hci", key_matrix_rows, key_matrix_rows, precision=peak_value)
    strict_part = jnp.where(strictly[None], ratios * products * write_rate[:, :, None], 0.0)
    system = strict_part + jnp.eye(length, dtype=jnp.float32)
    decay_factors = jnp.exp(cumulative)
    right_side = jnp.concatenate(
        [write_rate[..., None] * values, (write_rate * decay_factors)[..., None] * key_matrix_rows],
        axis=2,
    )
    solved = jax.scipy.linalg.solve_triangular(system, right_side, lower=True, unit_diagonal=True)
    state_update = solved[..., :value_width]
    mixing_weights = solved[..., value_width:]
    remaining_decay = jnp.exp(cumulative[:, -1:] - cumulative)[..., None] * key_matrix_rows
    identity = jnp.eye(key_matrix_rows.shape[2], dtype=jnp.float32)
    carry_map = decay_factors[:, -1][:, None, None] * identity - jnp.einsum(
        "hck,hcl->hkl", remaining_decay, mixing_weights, precision=peak_value
    )
    carried_increment = jnp.einsum(
        "snm,snt->smt", remaining_decay, state_update, precision=peak_value
    )
    scores = jnp.where(
        within[None],
        ratios * jnp.einsum("hck,hik->hci", query_vectors, key_matrix_rows, precision=peak_value),
        0.0,
    )
    return (carry_map, carried_increment, state_update, mixing_weights, decay_factors, scores)


def apply_map(square_matrix, recurrent_state):
    return jnp.einsum("ecw,ewj->ecj", square_matrix, recurrent_state, precision=peak_value)


def shards(
    span_query,
    span_key,
    span_value,
    span_beta_logit,
    span_logdecay,
    span_gate,
    norm_gain,
    prior_state,
    step_query,
    step_key,
    step_value,
    step_beta_logit,
    step_logdecay,
    step_gate,
    cache_key,
    cache_value,
    att_query,
    att_key,
    att_value,
    att_gate,
):
    ratio_heads = span_value.shape[1] // span_key.shape[1]
    tokens_local = span_value.shape[0]
    query_vectors = jnp.repeat(unit_rows(span_query) * DK ** (-0.5), ratio_heads, axis=1).transpose(
        1, 0, 2
    )
    key_matrix_rows = jnp.repeat(unit_rows(span_key), ratio_heads, axis=1).transpose(1, 0, 2)
    values = span_value.astype(jnp.float32).transpose(1, 0, 2)
    write_rate = jax.nn.sigmoid(span_beta_logit).T
    logdecay = span_logdecay.T
    carry_map, carried_increment, state_update, mixing_weights, decay_factors, scores = (
        block_transition(query_vectors, key_matrix_rows, values, write_rate, logdecay)
    )
    wide_count = lax.axis_size("wide")
    position = lax.axis_index("wide")

    def compose(earlier, later):
        return (apply_map(later[0], earlier[0]), apply_map(later[0], earlier[1]) + later[1])

    identity = (
        jnp.broadcast_to(jnp.eye(carry_map.shape[1], dtype=jnp.float32), carry_map.shape),
        jnp.zeros_like(carried_increment),
    )
    before_map, before_add = prefix((carry_map, carried_increment), "wide", compose, identity)
    incoming_state = apply_map(before_map, prior_state) + before_add
    leaving = apply_map(carry_map, incoming_state) + carried_increment
    prompt_state = broadcast(leaving, "wide", wide_count - 1)
    state_difference = state_update - jnp.einsum(
        "rey,ryt->ret", mixing_weights, incoming_state, precision=peak_value
    )
    span_kernel_body = decay_factors[..., None] * jnp.einsum(
        "rey,ryt->ret", query_vectors, incoming_state, precision=peak_value
    )
    span_kernel_body = span_kernel_body + jnp.einsum(
        "hci,hiv->hcv", scores, state_difference, precision=peak_value
    )
    span_kernel_body = span_kernel_body.transpose(1, 0, 2)
    span_out = (
        gated_norm(span_kernel_body, span_gate, norm_gain)
        .astype(jnp.bfloat16)
        .reshape(tokens_local, -1)
    )
    samples_local = step_value.shape[0]
    step_queries = jnp.repeat(unit_rows(step_query) * DK ** (-0.5), ratio_heads, axis=2)
    step_keys = jnp.repeat(unit_rows(step_key), ratio_heads, axis=2)
    step_values = step_value.astype(jnp.float32)
    step_rate = jax.nn.sigmoid(step_beta_logit)
    step_retention = jnp.exp(step_logdecay)
    recurrent_state = jnp.broadcast_to(prompt_state, (samples_local,) + prompt_state.shape)
    outputs = []
    for step_index in range(STEPS):
        recurrent_state, layer_output = delta_step(
            recurrent_state,
            step_queries[:, step_index],
            step_keys[:, step_index],
            step_values[:, step_index],
            step_rate[:, step_index],
            step_retention[:, step_index],
        )
        outputs.append(layer_output)
    step_core = jnp.stack(outputs, axis=1)
    step_out = (
        gated_norm(step_core, step_gate, norm_gain)
        .astype(jnp.bfloat16)
        .reshape(samples_local, STEPS, -1)
    )
    heads_local = att_query.shape[2]
    scaling = HD ** (-0.5)
    head_group = lax.axis_index("tp") * heads_local // (QH // KVH)
    group_keys = lax.dynamic_index_in_dim(cache_key, head_group, axis=1, keepdims=False)
    group_values = lax.dynamic_index_in_dim(cache_value, head_group, axis=1, keepdims=False)
    every_query = lax.all_gather(att_query, "wide", axis=0, tiled=True)
    sample_count = every_query.shape[0]
    query_rows = every_query.reshape(-1, every_query.shape[3])
    cache_scores = (
        jnp.einsum("rk,ck->rc", query_rows, group_keys, preferred_element_type=jnp.float32)
        * scaling
    )
    own_keys = lax.dynamic_index_in_dim(att_key, head_group, axis=2, keepdims=False)
    own_values = lax.dynamic_index_in_dim(att_value, head_group, axis=2, keepdims=False)
    own_scores = (
        jnp.einsum("sjak,sik->sjai", att_query, own_keys, preferred_element_type=jnp.float32)
        * scaling
    )
    causal = lax.broadcasted_iota(jnp.int32, (STEPS, STEPS), 0) >= lax.broadcasted_iota(
        jnp.int32, (STEPS, STEPS), 1
    )
    own_scores = jnp.where(causal[None, :, None, :], own_scores, -jnp.inf)
    local_max = jnp.max(cache_scores, axis=1).reshape(sample_count, STEPS, heads_local)
    offset = position * samples_local
    mine_before = lax.dynamic_slice_in_dim(local_max, offset, samples_local, 0)
    local_max = lax.dynamic_update_slice_in_dim(
        local_max, jnp.maximum(mine_before, jnp.max(own_scores, axis=3)), offset, 0
    )
    row_max = lax.pmax(local_max, "wide")
    cache_weights = jnp.exp(cache_scores - row_max.reshape(-1, 1)).astype(jnp.bfloat16)
    numerator = jnp.dot(cache_weights, group_values, preferred_element_type=jnp.float32)
    numerator = numerator.reshape(sample_count, STEPS, heads_local, -1)
    denominator = jnp.sum(cache_weights.astype(jnp.float32), axis=1).reshape(
        sample_count, STEPS, heads_local
    )
    numerator_all, denominator_all = lax.psum((numerator, denominator), "wide")
    numerator_mine = lax.dynamic_slice_in_dim(numerator_all, offset, samples_local, 0)
    denominator_mine = lax.dynamic_slice_in_dim(denominator_all, offset, samples_local, 0)
    max_mine = lax.dynamic_slice_in_dim(row_max, offset, samples_local, 0)
    own_weights = jnp.exp(own_scores - max_mine[..., None]).astype(jnp.bfloat16)
    numerator_mine = numerator_mine + jnp.einsum(
        "sjai,sik->sjak", own_weights, own_values, preferred_element_type=jnp.float32
    )
    denominator_mine = denominator_mine + jnp.sum(own_weights.astype(jnp.float32), axis=3)
    gate_values = jax.nn.sigmoid(att_gate.astype(jnp.float32))
    att_out = (numerator_mine / denominator_mine[..., None] * gate_values).astype(jnp.bfloat16)
    att_out = att_out.reshape(samples_local, STEPS, -1)
    return (span_out, step_out, recurrent_state, att_out)


def solution(mesh):
    in_specs = (
        P(("prompt", "wide"), "tp", None),
        P(("prompt", "wide"), "tp", None),
        P(("prompt", "wide"), "tp", None),
        P(("prompt", "wide"), "tp"),
        P(("prompt", "wide"), "tp"),
        P(("prompt", "wide"), "tp", None),
        P(),
        P(("prompt", "tp"), None, None),
        P(("prompt", "wide"), None, "tp", None),
        P(("prompt", "wide"), None, "tp", None),
        P(("prompt", "wide"), None, "tp", None),
        P(("prompt", "wide"), None, "tp"),
        P(("prompt", "wide"), None, "tp"),
        P(("prompt", "wide"), None, "tp", None),
        P(("prompt", "wide"), None, None),
        P(("prompt", "wide"), None, None),
        P(("prompt", "wide"), None, "tp", None),
        P(("prompt", "wide"), None, None, None),
        P(("prompt", "wide"), None, None, None),
        P(("prompt", "wide"), None, "tp", None),
    )
    out_specs = (
        P(("prompt", "wide"), "tp"),
        P(("prompt", "wide"), None, "tp"),
        P(("prompt", "wide"), "tp", None, None),
        P(("prompt", "wide"), None, "tp"),
    )
    return jax.shard_map(shards, mesh=mesh, in_specs=in_specs, out_specs=out_specs, check_vma=False)
```

profile of v0, /device:TPU:1, one launch (start us, length us, event | category | flops | bytes accessed | tf_op | source)
XLA Modules:
  0.0 902.0 jit_solution(3721533678242585864)
XLA Ops:
  9.3 2.2 reduce-window.6
  18.7 13.3 %select_add_fusion = f32[8,512,512]{2,1,0:T(8,128)} fusion(f32[512,512]{1,0:T(8,128)S(1)} %copy-done.18, f32[512,512]{1,0:T(8,128)S(1)} %copy-done.16, f32[8,512]{1,0:T(8,128)S(1)} %divide_bitcast_fusion, f32[8,512]{1,0:T(8,128)S(1)} %get-tuple-element.89, pred[512,512]{1,0:T(8,128)(4,1)S(1)} %copy-done.21, pred[512,512]{1,0:T(8,128)(4,1)S(1)} %copy-done.23, ...), kind=kOutput, calls=%fused_computation.13 | convolution fusion | flops 3238002688 | bytes 13402112 | tf_op jit(solution)/shard_map/hck,hik->hci/dot_general | solution.py:68
  32.0 16.6 %while.14 = (s32[]{:T(128)}, f32[8,512,512]{2,1,0:T(8,128)}, s32[4,2]{0,1:T(2,128)S(1)}, f32[4,8,128,128]{3,2,0,1:T(8,128)}, s32[]{:T(128)}) while((s32[]{:T(128)}, f32[8,512,512]{2,1,0:T(8,128)}, s32[4,2]{0,1:T(2,128)S(1)}, f32[4,8,128,128]{3,2,0,1:T(8,128)}, s32[]{:T(128)}) %tuple.68), condition=%wide.while_cond, body=%wide.while_body.sunk | while | flops 2 | bytes 1050209 | solution.py:76
  32.6 3.6 bitcast_dynamic-update-slice_fusion.2
  36.8 3.6 bitcast_dynamic-update-slice_fusion.2
  41.0 3.6 bitcast_dynamic-update-slice_fusion.2
  45.3 3.4 bitcast_dynamic-update-slice_fusion.2
  48.7 315.8 %custom-call.4 = f32[8,4,128,128]{2,3,1,0:T(8,128)} custom-call(f32[8,4,128,128]{3,2,1,0:T(8,128)} %bitcast.295), custom_call_target="InvertDiagBlocksLowerTriangular" | custom-call | tf_op jit(solution)/shard_map/jit(_solve_triangular)/vmap()/triangular_solve | solution.py:76
  364.5 1.7 bitcast_multiply_fusion.1
  368.9 2.1 convolution_subtract_fusion
  372.0 2.7 fusion.44
  375.7 3.7 fusion.39
  380.8 1.9 copy-done.2
  382.7 4.5 fusion.32
  387.5 6.5 fusion.48
  394.1 37.2 %all_gather.19 = bf16[16,4,4,256]{3,2,1,0:T(4,128)(2,1)S(1)} all-gather(bf16[1,4,4,256]{3,2,1,0:T(4,128)(2,1)S(1)} %copy-done.26), channel_id=1, replica_groups=mesh['wide'=16,'tp'=4,'prompt'=4] {'wide'}, dimensions={0}, use_global_device_ids=true | all-gather | bytes 139264 | tf_op jit(solution)/shard_map/all_gather | solution.py:191
  431.4 2.2 constant_dynamic-slice_fusion.7
  434.6 89.1 %pmax.7 = f32[16,4,4]{2,1,0:T(4,128)S(1)} all-reduce(f32[16,4,4]{2,1,0:T(4,128)S(1)} %constant_dynamic-update-slice_fusion), channel_id=1, replica_groups=mesh['wide'=16,'tp'=4,'prompt'=4] {'wide'}, use_global_device_ids=true, to_apply=%region_13.14 | all-reduce | flops 256 | bytes 2048 | tf_op jit(solution)/shard_map/pmax | solution.py:214
  526.3 2.2 constant_dynamic-slice_fusion.4
  534.5 96.3 %psum.23 = f32[16,4,4]{2,1,0:T(4,128)S(1)} all-reduce(f32[16,4,4]{2,1,0:T(4,128)S(1)} %reshape.638), channel_id=1, replica_groups=mesh['wide'=16,'tp'=4,'prompt'=4] {'wide'}, use_global_device_ids=true, to_apply=%region_16.17 | all-reduce | flops 256 | bytes 2048 | tf_op jit(solution)/shard_map/psum | solution.py:221
  632.4 8.8 fusion.117
  641.4 3.7 while.13
  641.4 1.9 convolution_add_fusion.4
  643.4 1.7 fusion.162
  645.8 4.9 fusion.34
  652.2 14.6 %fusion.7 = f32[8,512,128]{1,2,0:T(8,128)S(1)} fusion(f32[8,512,512]{2,1,0:T(8,128)} %fusion.117, f32[8,512]{1,0:T(8,128)S(1)} %get-tuple-element.89, pred[512,512]{1,0:T(8,128)(4,1)S(1)} %copy-done.22, f32[8,512,128]{2,1,0:T(8,128)} %fusion.34, f32[8,512,256]{2,1,0:T(8,128)} %copy-done.2), kind=kOutput, calls=%fused_computation.10 | convolution fusion | flops 3230138368 | bytes 14974976 | tf_op jit(solution)/shard_map/hci,hiv->hcv/dot_general | solution.py:153
  666.8 2.3 multiply_reduce_fusion
  671.5 211.3 %all-reduce.3.cloned.1.call-done = (f32[8,128,128]{2,1,0:T(8,128)}, f32[16,4,4,256]{3,2,1,0:T(4,128)}) async-done(((f32[8,128,128]{2,1,0:T(8,128)}, f32[16,4,4,256]{3,2,1,0:T(4,128)}), (f32[8,128,128]{2,1,0:T(8,128)}, f32[16,4,4,256]{3,2,1,0:T(4,128)})) %all-reduce.3.cloned.1.call-update) | async-done | bytes 786448 | tf_op jit(solution)/shard_map/psum | solution.py:31
  884.3 1.6 fusion.118
  885.9 1.7 fusion.106
  887.6 1.7 fusion.107
  892.1 1.5 fusion.75
  (173 shorter events, 39.4 us)
Async XLA Ops:
  7.2 424.3 %copy-start = (bf16[2048,2,256]{2,1,0:T(2,128)(2,1)S(1)}, bf16[2048,2,256]{2,1,0:T(2,128)(2,1)}, u32[]{:S(2)}) copy-start(bf16[2048,2,256]{2,1,0:T(2,128)(2,1)} %param.36) | copy-start | bytes 6291460
  7.2 6.3 copy-start.12
  7.2 634.1 %all-gather.7.cloned.1.call-start = ((), (), s32[]{:S(2)}) async-start(), calls=%async_computation.1 | async-start | bytes 8912896 | tf_op jit(solution)/shard_map/all_gather | solution.py:18
  16.3 2.3 copy-start.18
  16.3 2.3 copy-start.21
  16.3 2.4 copy-start.23
  16.5 15.6 %copy-start.6 = (f32[512,4,2,128]{3,0,2,1:T(8,128)}, f32[512,4,2,128]{3,0,2,1:T(8,128)S(1)}, u32[]{:S(2)}) copy-start(f32[512,4,2,128]{3,0,2,1:T(8,128)S(1)} %broadcast_in_dim.93) | copy-start | bytes 6291460
  367.7 13.1 %copy-start.3 = (f32[8,512,128]{2,1,0:T(8,128)}, f32[8,512,128]{2,1,0:T(8,128)S(1)}, u32[]{:S(2)}) copy-start(f32[8,512,128]{2,1,0:T(8,128)S(1)} %get-tuple-element.93) | copy-start | bytes 6291460
  380.8 2.0 copy-start.2
  387.2 254.0 %all-gather.5.cloned.1.call-start = ((), (), s32[]{:S(2)}) async-start(), calls=%async_computation | async-start | bytes 8912896 | tf_op jit(solution)/shard_map/all_gather | solution.py:18
  387.5 6.6 copy-start.26
  394.0 488.7 %all-reduce.3.cloned.1.call-start = ((), (), s32[]{:S(2)}) async-start(), calls=%async_computation.2 | async-start | bytes 1572864 | tf_op jit(solution)/shard_map/psum | solution.py:31
  524.3 2.0 copy-start.14
  526.3 2.2 copy-start.19
  528.5 1.8 copy-start.27
  528.6 1.8 copy-start.32
  528.6 1.8 copy-start.13
  531.9 99.0 %copy-start.30 = (bf16[1,4,2,256]{3,2,1,0:T(2,128)(2,1)S(1)}, bf16[1,4,2,256]{3,2,1,0:T(2,128)(2,1)}, u32[]{:S(2)}) copy-start(bf16[1,4,2,256]{3,2,1,0:T(2,128)(2,1)} %param.40) | copy-start | bytes 12292
  531.9 99.0 %copy-start.24 = (bf16[1,4,4,128]{3,2,1,0:T(4,128)(2,1)S(1)}, bf16[1,4,4,128]{3,2,1,0:T(4,128)(2,1)}, u32[]{:S(2)}) copy-start(bf16[1,4,4,128]{3,2,1,0:T(4,128)(2,1)} %param.31) | copy-start | bytes 12292
  531.9 99.0 %copy-start.25 = (bf16[1,4,4,128]{3,2,1,0:T(4,128)(2,1)S(1)}, bf16[1,4,4,128]{3,2,1,0:T(4,128)(2,1)}, u32[]{:S(2)}) copy-start(bf16[1,4,4,128]{3,2,1,0:T(4,128)(2,1)} %param.30) | copy-start | bytes 12292
  531.9 99.2 %copy-start.33 = (f32[1,4,8]{2,1,0:T(4,128)S(1)}, f32[1,4,8]{2,1,0:T(4,128)}, u32[]{:S(2)}) copy-start(f32[1,4,8]{2,1,0:T(4,128)} %param.33) | copy-start | bytes 388
  631.6 9.7 %copy-start.4 = (f32[512,4,2,128]{3,0,2,1:T(8,128)}, f32[512,4,2,128]{3,0,2,1:T(8,128)S(1)}, u32[]{:S(2)}) copy-start(f32[512,4,2,128]{3,0,2,1:T(8,128)S(1)} %broadcast_in_dim.91) | copy-start | bytes 6291460
  641.3 3.7 copy-start.20
  645.7 4.9 copy-start.8
  645.8 4.9 copy-start.9
  652.2 14.6 %copy-start.5 = (f32[512,4,2,128]{3,0,2,1:T(8,128)S(1)}, f32[512,4,2,128]{3,0,2,1:T(8,128)}, u32[]{:S(2)}) copy-start(f32[512,4,2,128]{3,0,2,1:T(8,128)} %copy-done.4) | copy-start | bytes 6291460
  666.8 2.4 copy-start.11
  666.8 2.3 copy-start.31
  670.0 212.8 %copy-start.34 = (bf16[1,4,4,256]{3,2,1,0:T(4,128)(2,1)S(1)}, bf16[1,4,4,256]{3,2,1,0:T(4,128)(2,1)}, u32[]{:S(2)}) copy-start(bf16[1,4,4,256]{3,2,1,0:T(4,128)(2,1)} %param.41) | copy-start | bytes 24580
  882.7 6.6 copy-start.10
  890.2 5.0 copy-start.1
  890.8 3.8 copy-start.28
  (6 other events, 8.2 us)
Sparse Core Ops, SparseCore 0:
  387.3 113.7 all-gather.6
  504.4 103.9 all-gather.4
  652.3 230.4 all-reduce.2
where the time goes:
time: 910 us; the launch traced here: 902 us
  other arithmetic  333 us (37%)
  blocking collectives  223 us (25%)
  waiting for transfers between devices  211 us (23%)
  matrix products  83.8 us (9%)
  local copies, waits for them, and re-layouts  36.1 us (4%)
  between operations  14.8 us (2%)
    another operation x6, other arithmetic, block_transition(): jax.scipy.linalg.solve_triangular(system, right_side, lower=True, unit_di...  319 us
    psum x1, waiting for transfers between devices, broadcast(): return lax.psum(jnp.where(mine, array, jnp.zeros_like(array)), axis)  211 us
    psum x1, blocking collectives, shards(): numerator_all, denominator_all = lax.psum((numerator, denominator), 'wide')  96.3 us
    pmax x1, blocking collectives, shards(): row_max = lax.pmax(local_max, 'wide')  89.1 us
    all_gather x1, blocking collectives, shards(): every_query = lax.all_gather(att_query, 'wide', axis=0, tiled=True)  37.2 us
  transfers between devices with their start and end apart: 3, of which 1 were waited for; matrix products, arithmetic and copies ran while one was open for 5% of the time, Pallas kernels for 0%

commit v1 on v0

v1 whole, which is shorter than its diff:
```python
import functools

import jax
import jax.numpy as jnp
from jax import lax
from jax.experimental import pallas as pl
from jax.experimental.pallas import tpu as pltpu
from jax.sharding import PartitionSpec as P

F32 = jnp.float32
BF16 = jnp.bfloat16
MESH = pl.DeviceIdType.MESH
EPS = 1e-6
C = 128
D = 128
HEADS = 8
KHEADS = 4
TOK = 512
NCH = TOK // C
HALF = 8
WIDE = 16
NEG = -1e30


def dot(a, b):
    return lax.dot_general(a, b, (((1,), (0,)), ((), ())), preferred_element_type=F32)


def dot_nt(a, b):
    return lax.dot_general(a, b, (((1,), (1,)), ((), ())), preferred_element_type=F32)


def dot_tn(a, b):
    return lax.dot_general(a, b, (((0,), (0,)), ((), ())), preferred_element_type=F32)


def split(x):
    hi = x.astype(BF16)
    return hi, (x - hi.astype(F32)).astype(BF16)


def sigmoid(x):
    return 1.0 / (1.0 + jnp.exp(-x))


def span_kernel(q_ref, k_ref, v_ref, s_ref, wire_ref, o_ref, g_ref, qf, kf, vf):
    qf[...] = q_ref[...].astype(F32)
    kf[...] = k_ref[...].astype(F32)
    vf[...] = v_ref[...].astype(F32)
    row = lax.broadcasted_iota(jnp.int32, (C, C), 0)
    col = lax.broadcasted_iota(jnp.int32, (C, C), 1)
    upper = (row <= col).astype(F32)

    def head(kh, _):
        rp = [None, None]
        acc = [None, None]
        for c in range(NCH):
            k32 = kf[pl.ds(c * C * KHEADS + kh, C, stride=KHEADS), :]
            q32 = qf[pl.ds(c * C * KHEADS + kh, C, stride=KHEADS), :]
            k16 = k32.astype(BF16)
            q16 = q32.astype(BF16)
            kt16 = k32.T.astype(BF16)
            kk = dot(k16, kt16)
            qk = dot(q16, kt16)
            eye = jnp.where(row == col, kk, 0.0)
            rk_row = lax.rsqrt(jnp.sum(eye, axis=0, keepdims=True) + EPS)
            rk = lax.rsqrt(jnp.sum(k32 * k32, axis=1, keepdims=True) + EPS)
            rq = lax.rsqrt(jnp.sum(q32 * q32, axis=1, keepdims=True) + EPS) * (D**-0.5)
            kkn = kk * rk * rk_row
            qkn = qk * rq * rk_row
            rows = s_ref[kh, :, c * C : (c + 1) * C]
            g_rows = lax.dot_general(
                rows, upper, (((1,), (0,)), ((), ())),
                precision=lax.Precision.HIGHEST, preferred_element_type=F32,
            )
            pick = lax.broadcasted_iota(jnp.int32, (8, C), 0) < 2
            mixed = jnp.where(pick, g_rows, sigmoid(rows))
            cols = mixed.T
            for e in range(2):
                g_row = g_rows[e : e + 1, :]
                g = cols[:, e : e + 1]
                b = cols[:, 2 + e : 3 + e]
                ratio = jnp.exp(jnp.where(row >= col, g - g_row, NEG))
                low = jnp.where(row > col, ratio * kkn * b, 0.0)
                sc = ratio * qkn
                near = jnp.where((row >> 1) == (col >> 1), low, 0.0)
                inv = -near
                for lg in range(1, 7):
                    off = jnp.where(
                        ((row >> (lg + 1)) == (col >> (lg + 1))) & ((row >> lg) != (col >> lg)),
                        low, 0.0,
                    )
                    inv16 = inv.astype(BF16)
                    y = off + dot(inv16, off.astype(BF16))
                    inv = inv - (y + dot(y.astype(BF16), inv16))
                eg = jnp.exp(g)
                g_end = g[C - 1 : C, :]
                e_end = jnp.exp(g_end)
                v32 = vf[pl.ds(c * C * HEADS + 2 * kh + e, C, stride=HEADS), :]
                rhs = jnp.concatenate([b * v32, (b * eg * rk) * k32], axis=1)
                x = rhs + dot(inv.astype(BF16), rhs.astype(BF16))
                u0, w = x[:, :D], x[:, D:]
                if c == 0:
                    uw = jnp.concatenate([u0, -w], axis=1)
                    base = None
                else:
                    rp16 = rp[e].astype(BF16)
                    wrp = dot(w.astype(BF16), rp16)
                    uw = jnp.concatenate(
                        [u0 - wrp[:, :D], -(acc[e] * w + wrp[:, D:])], axis=1
                    )
                    base = (eg * rq) * dot(q16, rp16)
                sch, scl = split(sc)
                uh, ul = split(uw)
                og = dot(sch, uh) + dot(scl, uh) + dot(sch, ul)
                if base is not None:
                    og = og + base
                direct = (eg * rq) if c == 0 else (eg * rq) * acc[e]
                hd = 2 * kh + e
                o_ref[hd, c * C : (c + 1) * C, :] = og[:, :D]
                gh, gl = split(og[:, D:] + direct * q32)
                g_ref[hd, c * C : (c + 1) * C, :D] = gh
                g_ref[hd, c * C : (c + 1) * C, D:] = gl
                sh, sl = split((jnp.exp(g_end - g) * rk) * uw)
                add = dot(kt16, sh) + dot(kt16, sl)
                if c == 0:
                    rp[e] = add
                    acc[e] = e_end
                else:
                    rp[e] = e_end * rp[e] + add
                    acc[e] = e_end * acc[e]
        for e in range(2):
            hd = 2 * kh + e
            bh, bl = split(rp[e][:, :D])
            wire_ref[hd, 0:C, 0:D] = rp[e][:, D:].astype(BF16)
            wire_ref[hd, 0:C, D : 2 * D] = bh
            wire_ref[hd, 0:C, 2 * D : 3 * D] = bl
            a = jnp.broadcast_to(acc[e], (16, 3 * D))
            a0 = a.astype(BF16).astype(F32)
            a1 = (a - a0).astype(BF16).astype(F32)
            a2 = a - a0 - a1
            lane = lax.broadcasted_iota(jnp.int32, (16, 3 * D), 1)
            wire_ref[hd, C : C + 16, :] = jnp.where(
                lane < D, a0, jnp.where(lane < 2 * D, a1, a2)
            ).astype(BF16)
        return 0

    lax.fori_loop(0, KHEADS, head, 0)


def span_local(q, k, v, scal):
    vm = pl.BlockSpec(memory_space=pltpu.VMEM)
    return pl.pallas_call(
        span_kernel,
        out_shape=(
            jax.ShapeDtypeStruct((HEADS, C + 16, 3 * D), BF16),
            jax.ShapeDtypeStruct((HEADS, TOK, D), F32),
            jax.ShapeDtypeStruct((HEADS, TOK, 2 * D), BF16),
        ),
        in_specs=[vm] * 4,
        out_specs=(vm, vm, vm),
        scratch_shapes=[
            pltpu.VMEM((TOK * KHEADS, D), F32),
            pltpu.VMEM((TOK * KHEADS, D), F32),
            pltpu.VMEM((TOK * HEADS, D), F32),
        ],
        compiler_params=pltpu.CompilerParams(vmem_limit_bytes=40 * 2**20),
        cost_estimate=pl.CostEstimate(flops=8 * 10**9, bytes_accessed=8 * 2**20, transcendentals=0),
        name="span_local",
    )(q, k, v, scal)


def attention_kernel(q_ref, k_ref, v_ref, m_ref, sc_ref):
    sc_ref[...] = dot_nt(q_ref[...], k_ref[...]) * (256**-0.5)
    scores = sc_ref[...]
    top = jnp.max(scores, axis=1, keepdims=True)
    w = jnp.exp(scores - top).astype(BF16)
    total = jnp.sum(w.astype(F32), axis=1, keepdims=True)
    out = dot(w, v_ref[...]) / total
    level = top + jnp.log(total)
    l0 = level.astype(BF16).astype(F32)
    l1 = (level - l0).astype(BF16).astype(F32)
    l2 = level - l0 - l1
    lane = lax.broadcasted_iota(jnp.int32, (256, 256), 1)
    packed = jnp.where(lane < 64, l0, jnp.where(lane < 128, l1, l2)).astype(BF16)
    out = out.astype(BF16)
    for s in range(WIDE):
        m_ref[s, 0:16, :] = out[s * 16 : (s + 1) * 16, :]
        m_ref[s, 16:32, :] = packed[s * 16 : (s + 1) * 16, :]


def attention_local(q, k, v):
    vm = pl.BlockSpec(memory_space=pltpu.VMEM)
    return pl.pallas_call(
        attention_kernel,
        out_shape=jax.ShapeDtypeStruct((WIDE, 32, 256), BF16),
        in_specs=[vm] * 3,
        out_specs=vm,
        scratch_shapes=[pltpu.VMEM((256, 2048), F32)],
        compiler_params=pltpu.CompilerParams(vmem_limit_bytes=32 * 2**20),
        cost_estimate=pl.CostEstimate(flops=6 * 10**8, bytes_accessed=3 * 2**20, transcendentals=2**19),
        name="attention_local",
    )(q, k, v)


def exchange_kernel(
    wire_ref, prior_ref, att_ref, sin_ref, fin_ref, parts_ref,
    maps, ent, mul, mid, finp, last,
    att_s, att_r, map_s, map_r, sin_s, sin_r, fin_s, fin_r, z_s, z_r,
):
    w = lax.axis_index("wide")
    zh = w // HALF
    j = w % HALF

    barrier = pltpu.get_barrier_semaphore()
    for d in range(1, WIDE):
        pl.semaphore_signal(
            barrier, inc=1, device_id={"wide": (w + d) % WIDE}, device_id_type=MESH
        )
    pl.semaphore_wait(barrier, WIDE - 1)

    def peer(d):
        return zh * HALF + (j + d) % HALF

    map_copies = []
    for d in range(1, HALF):
        to = (j + d) % HALF
        copy = pltpu.make_async_remote_copy(
            src_ref=wire_ref.at[to], dst_ref=maps.at[j],
            send_sem=map_s.at[d], recv_sem=map_r.at[d],
            device_id={"wide": peer(d)}, device_id_type=MESH,
        )
        copy.start()
        map_copies.append(copy)
    att_copies = []
    for d in range(1, WIDE):
        to = (w + d) % WIDE
        copy = pltpu.make_async_remote_copy(
            src_ref=att_ref.at[to], dst_ref=parts_ref.at[w],
            send_sem=att_s.at[d], recv_sem=att_r.at[d],
            device_id={"wide": to}, device_id_type=MESH,
        )
        copy.start()
        att_copies.append(copy)
    maps[j] = wire_ref[j]
    parts_ref[w] = att_ref[w]
    for copy in map_copies:
        copy.wait_recv()

    first = jnp.where(zh == 0, 1.0, 0.0)
    ent[0] = jnp.concatenate([prior_ref[j] * first, jnp.zeros((D, D), F32)], axis=1)
    mul[0] = jnp.ones((8, D), F32)

    def link(i, _):
        m16 = maps[i, 0:C, 0:D]
        add = maps[i, 0:C, D : 2 * D].astype(F32) + maps[i, 0:C, 2 * D : 3 * D].astype(F32)
        ar = maps[i, C : C + 16, :].astype(F32)
        a = (ar[0:8, 0:D] + ar[0:8, D : 2 * D]) + ar[0:8, 2 * D : 3 * D]
        x = ent[i]
        xh, xl = split(x)
        mx = dot(m16, xh) + dot(m16, xl)
        acc = mul[i]
        a1 = a[0:1, :]
        r = a1 * x[:, :D] + mx[:, :D] + add
        p = a1 * x[:, D:] + mx[:, D:] + acc[0:1, :] * m16.astype(F32)
        ent[i + 1] = jnp.concatenate([r, p], axis=1)
        mul[i + 1] = a * acc
        return 0

    lax.fori_loop(0, HALF, link, 0)

    @pl.when(zh == 0)
    def _():
        last[...] = ent[HALF, :, 0:D]
        copy = pltpu.make_async_remote_copy(
            src_ref=last, dst_ref=mid, send_sem=z_s.at[0], recv_sem=z_r.at[0],
            device_id={"wide": j + HALF}, device_id_type=MESH,
        )
        copy.start()
        copy.wait_send()

    @pl.when(zh == 1)
    def _():
        pltpu.make_async_remote_copy(
            src_ref=last, dst_ref=mid, send_sem=z_s.at[0], recv_sem=z_r.at[0],
            device_id={"wide": j}, device_id_type=MESH,
        ).wait_recv()
        s = mid[...]
        sh, sl = split(s)
        both = jnp.concatenate([sh, sl], axis=1)

        def enter(i, _):
            x = ent[i]
            ph, pl_ = split(x[:, D:])
            y = dot(ph, both)
            ent[i, :, 0:D] = (
                x[:, :D] + mul[i, 0:1, :] * s + y[:, :D] + y[:, D:] + dot(pl_, sh)
            )
            return 0

        lax.fori_loop(0, HALF + 1, enter, 0)
        finp[...] = ent[HALF, :, 0:D]

    sin_copies = []
    stage = maps_stage = None
    for d in range(1, HALF):
        to = (j + d) % HALF
        copy = pltpu.make_async_remote_copy(
            src_ref=ent.at[to, :, pl.ds(0, D)], dst_ref=sin_ref.at[j],
            send_sem=sin_s.at[d], recv_sem=sin_r.at[d],
            device_id={"wide": peer(d)}, device_id_type=MESH,
        )
        copy.start()
        sin_copies.append(copy)
    sin_ref[j] = ent[j, :, 0:D]

    @pl.when(zh == 1)
    def _():
        copy = pltpu.make_async_remote_copy(
            src_ref=finp, dst_ref=finp, send_sem=z_s.at[1], recv_sem=z_r.at[1],
            device_id={"wide": j}, device_id_type=MESH,
        )
        copy.start()
        copy.wait_send()

    @pl.when(zh == 0)
    def _():
        pltpu.make_async_remote_copy(
            src_ref=finp, dst_ref=finp, send_sem=z_s.at[1], recv_sem=z_r.at[1],
            device_id={"wide": j + HALF}, device_id_type=MESH,
        ).wait_recv()

    fin_copies = []
    for d in range(1, HALF):
        copy = pltpu.make_async_remote_copy(
            src_ref=finp, dst_ref=fin_ref.at[j],
            send_sem=fin_s.at[d], recv_sem=fin_r.at[d],
            device_id={"wide": peer(d)}, device_id_type=MESH,
        )
        copy.start()
        fin_copies.append(copy)
    fin_ref[j] = finp[...]
    for copy in map_copies:
        copy.wait_send()
    for copy in att_copies + sin_copies + fin_copies:
        copy.wait()


def exchange(wire, prior, att):
    vm = pl.BlockSpec(memory_space=pltpu.VMEM)
    sem = pltpu.SemaphoreType.DMA
    return pl.pallas_call(
        exchange_kernel,
        out_shape=(
            jax.ShapeDtypeStruct((HEADS, D, D), F32),
            jax.ShapeDtypeStruct((HEADS, D, D), F32),
            jax.ShapeDtypeStruct((WIDE, 32, 256), BF16),
        ),
        in_specs=[vm] * 3,
        out_specs=(vm, vm, vm),
        scratch_shapes=[
            pltpu.VMEM((HALF, C + 16, 3 * D), BF16),
            pltpu.VMEM((HALF + 1, D, 2 * D), F32),
            pltpu.VMEM((HALF + 1, 8, D), F32),
            pltpu.VMEM((D, D), F32),
            pltpu.VMEM((D, D), F32),
            pltpu.VMEM((D, D), F32),
            sem((WIDE,)), sem((WIDE,)),
            sem((HALF,)), sem((HALF,)),
            sem((HALF,)), sem((HALF,)),
            sem((HALF,)), sem((HALF,)),
            sem((2,)), sem((2,)),
        ],
        compiler_params=pltpu.CompilerParams(
            collective_id=0, has_side_effects=True, vmem_limit_bytes=32 * 2**20
        ),
        name="exchange",
    )(wire, prior, att)


def output_kernel(
    o_ref, g_ref, sin_ref, fin_ref, gate_ref, gain_ref,
    kq_ref, sv_ref, sb_ref, sd_ref, sg_ref,
    parts_ref, aq_ref, ak_ref, av_ref, ag_ref,
    out_ref, step_ref, state_ref, att_ref,
    gatef, res, uscr,
):
    gain = gain_ref[...]
    gatef[...] = gate_ref[...].astype(F32)

    def head(h, _):
        s = sin_ref[h]
        sh, sl = split(s)
        both = jnp.concatenate([sh, sl], axis=1)
        both = jnp.concatenate([both, both], axis=0)
        y = dot(g_ref[h], both)
        o = o_ref[h] + (y[:, :D] + y[:, D:])
        scale = lax.rsqrt(jnp.mean(o * o, axis=1, keepdims=True) + EPS)
        z = gatef[pl.ds(h, TOK, stride=HEADS), :]
        r = (o * scale * gain * (z * sigmoid(z))).astype(BF16)
        out_ref[:, pl.ds(pl.multiple_of(h * D, D), D)] = r
        return 0

    lax.fori_loop(0, HEADS, head, 0)

    def recall(h, _):
        sh, sl = split(fin_ref[h])
        both = jnp.concatenate([sh, sl], axis=1)
        y = dot(kq_ref[h].astype(BF16), both)
        res[pl.ds(pl.multiple_of(h * 8, 8), 8), :] = y[:, :D] + y[:, D:]
        return 0

    lax.fori_loop(0, HEADS, recall, 0)
    kraw = [kq_ref[:, i, :] for i in range(4)]
    qraw = [kq_ref[:, 4 + i, :] for i in range(4)]
    rk = [lax.rsqrt(jnp.sum(x * x, axis=1, keepdims=True) + EPS) for x in kraw]
    rq = [lax.rsqrt(jnp.sum(x * x, axis=1, keepdims=True) + EPS) * (D**-0.5) for x in qraw]
    kn = [x * r for x, r in zip(kraw, rk)]
    qn = [x * r for x, r in zip(qraw, rq)]
    beta = sigmoid(sb_ref[...])
    ld = sd_ref[...]
    cum = [ld[:, 0:1]]
    for i in range(1, 4):
        cum.append(cum[-1] + ld[:, i : i + 1])
    us = []
    for i in range(4):
        ks = res[pl.ds(i, HEADS, stride=8), :] * (rk[i] * jnp.exp(cum[i]))
        u = sv_ref[i].astype(F32) - ks
        for p in range(i):
            kk = jnp.sum(kn[i] * kn[p], axis=1, keepdims=True)
            u = u - (jnp.exp(cum[i] - cum[p]) * kk) * us[p]
        u = beta[:, i : i + 1] * u
        us.append(u)
        o = res[pl.ds(4 + i, HEADS, stride=8), :] * (rq[i] * jnp.exp(cum[i]))
        for p in range(i + 1):
            qk = jnp.sum(qn[i] * kn[p], axis=1, keepdims=True)
            o = o + (jnp.exp(cum[i] - cum[p]) * qk) * us[p]
        scale = lax.rsqrt(jnp.mean(o * o, axis=1, keepdims=True) + EPS)
        z = sg_ref[i].astype(F32)
        step_ref[i] = (o * scale * gain * (z * sigmoid(z))).astype(BF16)
    for i in range(4):
        uscr[pl.ds(i, HEADS, stride=8), :] = us[i] * (jnp.exp(cum[3] - cum[i]) * rk[i])
        uscr[pl.ds(4 + i, HEADS, stride=8), :] = jnp.zeros((HEADS, D), F32)
    decay = jnp.broadcast_to(jnp.exp(cum[3]), (HEADS, D))
    for h in range(HEADS):
        uh, ul = split(uscr[h * 8 : (h + 1) * 8, :])
        both = jnp.concatenate([uh, ul], axis=1)
        y = dot_tn(kq_ref[h].astype(BF16), both)
        state_ref[h] = decay[h : h + 1, :] * fin_ref[h] + (y[:, :D] + y[:, D:])

    tp = lax.axis_index("tp")
    group = tp // 2
    aq = aq_ref[...]
    own = dot_nt(aq, ak_ref[...]) * (256**-0.5)
    r = lax.broadcasted_iota(jnp.int32, (16, 8), 0) // 4
    cc = lax.broadcasted_iota(jnp.int32, (16, 8), 1)
    own = jnp.where((cc % 2 == group) & (cc // 2 <= r), own, NEG)
    top = jnp.max(own, axis=1, keepdims=True)
    levels = []
    for s in range(WIDE):
        packed = parts_ref[s, 16:32, :].astype(F32)
        lv = (packed[:, 0:1] + packed[:, 64:65]) + packed[:, 128:129]
        levels.append(lv)
        top = jnp.maximum(top, lv)
    pw = jnp.exp(own - top).astype(BF16)
    den = jnp.sum(pw.astype(F32), axis=1, keepdims=True)
    num = dot(pw, av_ref[...])
    for s in range(WIDE):
        wt = jnp.exp(levels[s] - top)
        den = den + wt
        num = num + wt * parts_ref[s, 0:16, :].astype(F32)
    att_ref[...] = (num / den * sigmoid(ag_ref[...].astype(F32))).astype(BF16)


def outputs(*args):
    vm = pl.BlockSpec(memory_space=pltpu.VMEM)
    return pl.pallas_call(
        output_kernel,
        out_shape=(
            jax.ShapeDtypeStruct((TOK, HEADS * D), BF16),
            jax.ShapeDtypeStruct((4, HEADS, D), BF16),
            jax.ShapeDtypeStruct((HEADS, D, D), F32),
            jax.ShapeDtypeStruct((16, 256), BF16),
        ),
        in_specs=[vm] * 16,
        out_specs=(vm,) * 4,
        scratch_shapes=[
            pltpu.VMEM((TOK * HEADS, D), F32),
            pltpu.VMEM((64, D), F32),
            pltpu.VMEM((64, D), F32),
        ],
        compiler_params=pltpu.CompilerParams(vmem_limit_bytes=40 * 2**20),
        name="outputs",
    )(*args)


def shards(
    span_query, span_key, span_value, span_beta_logit, span_logdecay, span_gate,
    norm_gain, prior_state,
    step_query, step_key, step_value, step_beta_logit, step_logdecay, step_gate,
    cache_key, cache_value, att_query, att_key, att_value, att_gate,
):
    q = span_query.reshape(TOK * KHEADS, D)
    k = span_key.reshape(TOK * KHEADS, D)
    v = span_value.reshape(TOK * HEADS, D)
    gate = span_gate.reshape(TOK * HEADS, D)
    ldt = span_logdecay.T.reshape(KHEADS, 2, TOK)
    blt = span_beta_logit.T.reshape(KHEADS, 2, TOK)
    scal = jnp.concatenate([ldt, blt, jnp.zeros((KHEADS, 4, TOK), F32)], axis=1)
    every_query = lax.all_gather(att_query, "wide", axis=0, tiled=True).reshape(256, 256)
    group = lax.axis_index("tp") // 2
    keys = lax.dynamic_index_in_dim(cache_key, group, axis=1, keepdims=False)
    values = lax.dynamic_index_in_dim(cache_value, group, axis=1, keepdims=False)
    wire, o0, g = span_local(q, k, v, scal)
    att = attention_local(every_query, keys, values)
    sin, fin, parts = exchange(wire, prior_state, att)
    kq = jnp.repeat(
        jnp.concatenate([step_key[0], step_query[0]], axis=0).transpose(1, 0, 2), 2, axis=0
    ).astype(F32)
    out, step, state, att_out = outputs(
        o0, g, sin, fin, gate, norm_gain.reshape(1, D),
        kq, step_value[0], step_beta_logit[0].T, step_logdecay[0].T, step_gate[0],
        parts, att_query.reshape(16, 256), att_key.reshape(8, 256), att_value.reshape(8, 256),
        att_gate.reshape(16, 256),
    )
    return (
        out, step.reshape(1, 4, HEADS * D), state[None], att_out.reshape(1, 4, 1024)
    )


def solution(mesh):
    tok = P(("prompt", "wide"), "tp", None)
    tok2 = P(("prompt", "wide"), "tp")
    stp = P(("prompt", "wide"), None, "tp", None)
    stp2 = P(("prompt", "wide"), None, "tp")
    in_specs = (
        tok, tok, tok, tok2, tok2, tok, P(), P(("prompt", "tp"), None, None),
        stp, stp, stp, stp2, stp2, stp,
        P(("prompt", "wide"), None, None), P(("prompt", "wide"), None, None),
        stp, P(("prompt", "wide"), None, None, None), P(("prompt", "wide"), None, None, None), stp,
    )
    out_specs = (
        P(("prompt", "wide"), "tp"),
        stp2,
        P(("prompt", "wide"), "tp", None, None),
        stp2,
    )
    return jax.shard_map(shards, mesh=mesh, in_specs=in_specs, out_specs=out_specs, check_vma=False)
```

time: 910 us -> 159 us (0.17)
  other arithmetic: 333 us -> 0.79 us
  waiting for transfers between devices: 211 us -> 0 us
  blocking collectives: 223 us -> 35.3 us
  Pallas kernels: 0 us -> 108 us
  matrix products: 83.8 us -> 0 us
  local copies, waits for them, and re-layouts: 36.1 us -> 13.3 us
  between operations: 14.8 us -> 0.85 us
    another operation x8 -> x0, other arithmetic: 321 us -> none  [the longest x6 319 us: block_transition(): jax.scipy.linalg.solve_triangular(system, right_side, lower=True, unit_di...]
    psum x1 -> x0, waiting for transfers between devices: 211 us -> none  [broadcast(): return lax.psum(jnp.where(mine, array, jnp.zeros_like(array)), axis)]
    pallas_call x0 -> x4, Pallas kernels: none -> 108 us  [the longest x1 64.3 us: span_local(): pl.pallas_call(span_kernel, out_shape=(jax.ShapeDtypeStruct((HEADS, C + 1...]
    psum x1 -> x0, blocking collectives: 96.3 us -> none  [shards(): numerator_all, denominator_all = lax.psum((numerator, denominator), 'wide')]
    pmax x1 -> x0, blocking collectives: 89.1 us -> none  [shards(): row_max = lax.pmax(local_max, 'wide')]
    dot_general x23 -> x0, matrix products: 71.2 us -> none  [the longest x1 14.6 us: shards(): jnp.einsum('hci,hiv->hcv', scores, state_difference, precision=peak_value)]
    another operation x16 -> x0, local copies, waits for them, and re-layouts: 16.8 us -> none
    another operation x7 -> x0, matrix products: 12.6 us -> none  [block_transition(): jax.scipy.linalg.solve_triangular(system, right_side, lower=True, unit_di...]
  transfers between devices with their start and end apart: 3 -> 0, of which waited for: 1 -> 0; matrix products, arithmetic and copies ran while one was open for 5% -> 0% of each run, Pallas kernels for 0% -> 0%
where the time goes in v1:
time: 159 us; the launch traced here: 158 us
  Pallas kernels  108 us (68%)
  blocking collectives  35.3 us (22%)
  local copies, waits for them, and re-layouts  13.3 us (8%)
    pallas_call x1, Pallas kernels, span_local(): pl.pallas_call(span_kernel, out_shape=(jax.ShapeDtypeStruct((HEADS, C + 1...  64.3 us
    pallas_call x1, Pallas kernels, exchange(): pl.pallas_call(exchange_kernel, out_shape=(jax.ShapeDtypeStruct((HEADS, D...  35.9 us
    all_gather x1, blocking collectives, shards(): lax.all_gather(att_query, 'wide', axis=0, tiled=True).reshape(256, 256)  35.3 us
    pallas_call x1, Pallas kernels, outputs(): pl.pallas_call(output_kernel, out_shape=(jax.ShapeDtypeStruct((TOK, HEADS...  5.87 us
    dynamic_slice x1, local copies, waits for them, and re-layouts, shards(): lax.dynamic_index_in_dim(cache_value, group, axis=1, keepdims=False)  5.72 us

profile of v1, /device:TPU:1, one launch (start us, length us, event | category | flops | bytes accessed | tf_op | source)
XLA Modules:
  0.0 158.0 jit_solution(10000048977518009250)
XLA Ops:
  0.7 0.1 pad.4.clone
  0.7 0.8 copy.35
  1.5 0.8 copy.36
  2.2 0.7 reshape.61.ak_ref
  2.9 0.7 reshape.62.av_ref
  3.6 0.7 reshape.63.ag_ref
  4.3 0.7 reshape.60.aq_ref
  5.0 0.7 reshape.56
  5.8 0.7 reshape.55
  6.5 0.7 convert_bitcast_fusion
  7.3 0.1 maximum_maximum_fusion.s_ref
  7.3 35.3 %all_gather.3 = bf16[16,4,4,256]{3,2,1,0:T(4,128)(2,1)S(1)} all-gather(bf16[1,4,4,256]{3,2,1,0:T(4,128)(2,1)} %param.36), channel_id=1, replica_groups=mesh['wide'=16,'tp'=4,'prompt'=4] {'wide'}, dimensions={0}, use_global_device_ids=true | all-gather | bytes 139264 | tf_op jit(solution)/shard_map/all_gather | solution.py:510
  42.7 5.7 %constant_dynamic-slice_fusion = (bf16[2048,1,256]{2,1,0:T(2,128)(2,1)S(1)}, bf16[2048,1,256]{2,1,0:T(2,128)(2,1)S(1)}) fusion(bf16[2048,2,256]{2,1,0:T(2,128)(2,1)} %param.35, s32[]{:T(128)S(6)} %select_n.11, bf16[2048,2,256]{2,1,0:T(2,128)(2,1)} %param.34), kind=kLoop, calls=%fused_computation.4 | loop fusion | bytes 4194308 | tf_op jit(solution)/shard_map/jit(dynamic_index_in_dim)/dynamic_slice | solution.py:513
  48.4 0.2 copy.41
  48.6 0.0 copy-start.5
  48.6 0.0 copy-start.6
  48.6 0.0 copy-start.7
  48.6 0.2 copy.42
  48.8 1.7 %attention_local.1.att_ref = bf16[16,32,256]{2,1,0:T(8,128)(2,1)S(1)} custom-call(bf16[256,256]{1,0:T(8,128)(2,1)S(1)} %reshape.57.q_ref, bf16[2048,256]{1,0:T(8,128)(2,1)S(1)} %bitcast.26, bf16[2048,256]{1,0:T(8,128)(2,1)S(1)} %bitcast.25), custom_call_target="tpu_custom_call" | custom-call | flops 600000000 | bytes 3145728 | tf_op jit(solution)/shard_map/attention_local/pallas_call | solution.py:194
  50.5 0.0 copy-done.5
  50.5 0.0 copy-done.6
  50.5 0.0 copy-done.7
  50.5 0.0 copy-start.1
  50.5 0.0 copy-start.2
  50.6 0.0 copy-start.3
  50.6 0.0 copy-start.4
  50.6 64.3 %span_local.1 = (bf16[8,144,384]{2,1,0:T(8,128)(2,1)S(1)}, f32[8,512,128]{2,1,0:T(8,128)S(1)}, bf16[8,512,256]{2,1,0:T(8,128)(2,1)S(1)}) custom-call(bf16[2048,128]{1,0:T(8,128)(2,1)S(1)} %bitcast.35, bf16[2048,128]{1,0:T(8,128)(2,1)S(1)} %bitcast.36, bf16[4096,128]{1,0:T(8,128)(2,1)S(1)} %bitcast.34, f32[4,8,512]{2,1,0:T(8,128)S(1)} %maximum_maximum_fusion.s_ref), custom_call_target="tpu_custom_call" | custom-call | flops 8000000000 | bytes 8388608 | tf_op jit(solution)/shard_map/span_local/pallas_call | solution.py:153
  114.9 0.0 copy-start
  114.9 35.9 %exchange.1 = (f32[8,128,128]{2,1,0:T(8,128)S(1)}, f32[8,128,128]{2,1,0:T(8,128)S(1)}, bf16[16,32,256]{2,1,0:T(8,128)(2,1)S(1)}) custom-call(bf16[8,144,384]{2,1,0:T(8,128)(2,1)S(1)} %get-tuple-element.16.wire_ref, f32[8,128,128]{2,1,0:T(8,128)S(1)} %copy-done.1, bf16[16,32,256]{2,1,0:T(8,128)(2,1)S(1)} %attention_local.1.att_ref), custom_call_target="tpu_custom_call" | custom-call | tf_op jit(solution)/shard_map/exchange/pallas_call | solution.py:352
  150.9 5.9 %outputs.1 = (bf16[512,1024]{1,0:T(8,128)(2,1)}, bf16[4,8,128]{2,1,0:T(8,128)(2,1)S(1)}, f32[8,128,128]{2,1,0:T(8,128)}, bf16[16,256]{1,0:T(8,128)(2,1)S(1)}) custom-call(f32[8,512,128]{2,1,0:T(8,128)S(1)} %get-tuple-element.14.o_ref, bf16[8,512,256]{2,1,0:T(8,128)(2,1)S(1)} %get-tuple-element.15.g_ref, f32[8,128,128]{2,1,0:T(8,128)S(1)} %get-tuple-element.17.sin_ref, ...), custom_call_target="tpu_custom_call" | custom-call | tf_op jit(solution)/shard_map/outputs/pallas_call | solution.py:477
  156.7 0.6 reshape.64
  157.3 0.6 reshape.65
  (9 shorter events, 0.1 us)
Async XLA Ops:
  48.6 1.9 %copy-start.5 = (bf16[512,8,128]{2,1,0:T(8,128)(2,1)S(1)}, bf16[512,8,128]{2,1,0:T(8,128)(2,1)}, u32[]{:S(2)}) copy-start(bf16[512,8,128]{2,1,0:T(8,128)(2,1)} %param.22) | copy-start | bytes 3145732
  48.6 1.9 %copy-start.6 = (bf16[512,4,128]{2,1,0:T(4,128)(2,1)S(1)}, bf16[512,4,128]{2,1,0:T(4,128)(2,1)}, u32[]{:S(2)}) copy-start(bf16[512,4,128]{2,1,0:T(4,128)(2,1)} %param.20) | copy-start | bytes 1572868
  48.6 1.9 %copy-start.7 = (bf16[512,4,128]{2,1,0:T(4,128)(2,1)S(1)}, bf16[512,4,128]{2,1,0:T(4,128)(2,1)}, u32[]{:S(2)}) copy-start(bf16[512,4,128]{2,1,0:T(4,128)(2,1)} %param.21) | copy-start | bytes 1572868
  50.5 64.3 %copy-start.1 = (f32[8,128,128]{2,1,0:T(8,128)S(1)}, f32[8,128,128]{2,1,0:T(8,128)}, u32[]{:S(2)}) copy-start(f32[8,128,128]{2,1,0:T(8,128)} %prior_ref.1) | copy-start | bytes 1572868
  50.5 100.3 %copy-start.2 = (bf16[1,4,8,128]{3,2,1,0:T(8,128)(2,1)S(1)}, bf16[1,4,8,128]{3,2,1,0:T(8,128)(2,1)}, u32[]{:S(2)}) copy-start(bf16[1,4,8,128]{3,2,1,0:T(8,128)(2,1)} %param.30) | copy-start | bytes 24580
  50.6 100.3 %copy-start.3 = (bf16[1,4,8,128]{3,2,1,0:T(8,128)(2,1)S(1)}, bf16[1,4,8,128]{3,2,1,0:T(8,128)(2,1)}, u32[]{:S(2)}) copy-start(bf16[1,4,8,128]{3,2,1,0:T(8,128)(2,1)} %param.33) | copy-start | bytes 24580
  50.6 100.3 %copy-start.4 = (f32[128]{0:T(128)S(1)}, f32[128]{0:T(128)}, u32[]{:S(2)}) copy-start(f32[128]{0:T(128)} %param.26) | copy-start | bytes 1540
  114.9 36.0 %copy-start = (bf16[512,8,128]{2,1,0:T(8,128)(2,1)S(1)}, bf16[512,8,128]{2,1,0:T(8,128)(2,1)}, u32[]{:S(2)}) copy-start(bf16[512,8,128]{2,1,0:T(8,128)(2,1)} %param.25) | copy-start | bytes 3145732

commit v2 on v1

v2 whole, which is shorter than its diff:
```python
import jax
import jax.numpy as jnp
from jax import lax
from jax.experimental import pallas as pl
from jax.experimental.pallas import tpu as pltpu
from jax.sharding import PartitionSpec as P

F32 = jnp.float32
BF16 = jnp.bfloat16
MESH = pl.DeviceIdType.MESH
EPS = 1e-6
C = 128
D = 128
HEADS = 8
KHEADS = 4
TOK = 512
NCH = TOK // C
HALF = 8
WIDE = 16
NEG = -1e30


def dot(a, b):
    return lax.dot_general(a, b, (((1,), (0,)), ((), ())), preferred_element_type=F32)


def dot_nt(a, b):
    return lax.dot_general(a, b, (((1,), (1,)), ((), ())), preferred_element_type=F32)


def dot_tn(a, b):
    return lax.dot_general(a, b, (((0,), (0,)), ((), ())), preferred_element_type=F32)


def split(x):
    hi = x.astype(BF16)
    return hi, (x - hi.astype(F32)).astype(BF16)


def sigmoid(x):
    return 1.0 / (1.0 + jnp.exp(-x))


def kernel(
    q_hbm, k_hbm, v_hbm, bl_ref, ld_ref, gate_hbm, gain_ref, prior_hbm,
    sq_ref, sk_ref, sv_ref, sb_ref, sd_ref, sg_ref,
    ck_hbm, cv_hbm, aq_ref, ak_ref, av_ref, ag_ref,
    out_ref, step_ref, state_ref, att_ref,
    qv, kv, vv, gv, ckv, cvv, prior,
    qf, kf, vf, cf, kc, vc, scores, scal,
    wire, maps, o0, gq, ent, mul, mid, fin_z,
    sin16, sin, finp, fin, own_q, all_q, msg, parts,
    kqs, res, uscr, sscr, a0s, a1s, own_k,
    load, q_s, q_r, att_s, att_r, map_s, map_r, sin_s, sin_r, fin_s, fin_r, z_s, z_r,
):
    w = lax.axis_index("wide")
    zh = w // HALF
    j = w % HALF
    group = lax.axis_index("tp") // 2

    loads = []
    for i, (src, dst) in enumerate((
        (ck_hbm, ckv), (cv_hbm, cvv), (q_hbm, qv), (k_hbm, kv), (v_hbm, vv), (gate_hbm, gv),
        (prior_hbm.at[j], prior),
    )):
        copy = pltpu.make_async_copy(src, dst, load.at[i])
        copy.start()
        loads.append(copy)

    barrier = pltpu.get_barrier_semaphore()
    for d in range(1, WIDE):
        pl.semaphore_signal(
            barrier, inc=1, device_id={"wide": (w + d) % WIDE}, device_id_type=MESH
        )
    for i in range(4):
        a0s[4 * i : 4 * i + 4, :] = aq_ref[0, i].astype(F32)
    own_q[...] = a0s[...].astype(BF16)
    pl.semaphore_wait(barrier, WIDE - 1)

    def remote(src, dst, ss, rs, to):
        return pltpu.make_async_remote_copy(
            src_ref=src, dst_ref=dst, send_sem=ss, recv_sem=rs,
            device_id={"wide": to}, device_id_type=MESH,
        )

    def map_copy(to, slot, device):
        return remote(wire.at[to], maps.at[slot], map_s.at[to], map_r.at[slot], device)

    q_copies = []
    for d in range(1, WIDE):
        copy = remote(own_q, all_q.at[w], q_s.at[d], q_r.at[d], (w + d) % WIDE)
        copy.start()
        q_copies.append(copy)
    all_q[w] = own_q[...]

    upper = (
        lax.broadcasted_iota(jnp.int32, (C, C), 0) <= lax.broadcasted_iota(jnp.int32, (C, C), 1)
    ).astype(F32)
    scal[...] = jnp.zeros_like(scal)
    for c in range(NCH):
        part = slice(c * C, (c + 1) * C)
        g8 = lax.dot_general(
            ld_ref[:, part], upper, (((1,), (0,)), ((), ())),
            precision=lax.Precision.HIGHEST, preferred_element_type=F32,
        )
        b8 = sigmoid(bl_ref[:, part])
        for kh in range(KHEADS):
            scal[kh, 0:2, part] = g8[2 * kh : 2 * kh + 2]
            scal[kh, 2:4, part] = b8[2 * kh : 2 * kh + 2]

    for load_copy, raw, cut in ((loads[0], ckv, kc), (loads[1], cvv, vc)):
        load_copy.wait()
        cf[...] = raw[...].astype(F32)
        cut[:, 0:128] = cf[pl.ds(group, 2048, stride=4), :].astype(BF16)
        cut[:, 128:256] = cf[pl.ds(2 + group, 2048, stride=4), :].astype(BF16)
    for copy in loads[2:]:
        copy.wait()
    qf[...] = qv[...].astype(F32)
    kf[...] = kv[...].astype(F32)
    vf[...] = vv[...].astype(F32)

    for copy in q_copies:
        copy.wait()
    scores[...] = dot_nt(all_q[...].reshape(256, 256), kc[...]) * (256**-0.5)
    sc = scores[...]
    top = jnp.max(sc, axis=1, keepdims=True)
    wt = jnp.exp(sc - top).astype(BF16)
    total = jnp.sum(wt.astype(F32), axis=1, keepdims=True)
    num = (dot(wt, vc[...]) / total).astype(BF16)
    level = top + jnp.log(total)
    l0 = level.astype(BF16).astype(F32)
    l1 = (level - l0).astype(BF16).astype(F32)
    l2 = level - l0 - l1
    lane = lax.broadcasted_iota(jnp.int32, (256, 256), 1)
    packed = jnp.where(lane < 64, l0, jnp.where(lane < 128, l1, l2)).astype(BF16)
    for s in range(WIDE):
        msg[s, 0:16, :] = num[s * 16 : (s + 1) * 16, :]
        msg[s, 16:32, :] = packed[s * 16 : (s + 1) * 16, :]
    att_copies = []
    for d in range(1, WIDE):
        to = (w + d) % WIDE
        copy = remote(msg.at[to], parts.at[w], att_s.at[d], att_r.at[d], to)
        copy.start()
        att_copies.append(copy)
    parts[w] = msg[w]

    row = lax.broadcasted_iota(jnp.int32, (C, C), 0)
    col = lax.broadcasted_iota(jnp.int32, (C, C), 1)

    def head(it, _):
        kh = (j // 2 + jnp.where(it == 0, 2, 0) + jnp.where(it == 1, 1, 0)
              + jnp.where(it == 2, 3, 0)) % KHEADS
        ks, qs, kts, cells = [], [], [], []
        for c in range(NCH):
            k32 = kf[pl.ds(c * C * KHEADS + kh, C, stride=KHEADS), :]
            q32 = qf[pl.ds(c * C * KHEADS + kh, C, stride=KHEADS), :]
            k16 = k32.astype(BF16)
            q16 = q32.astype(BF16)
            kt16 = k32.T.astype(BF16)
            kq = dot(jnp.concatenate([k16, q16], axis=0), kt16)
            kk, qk = kq[:C], kq[C:]
            eye = jnp.where(row == col, kk, 0.0)
            rk_row = lax.rsqrt(jnp.sum(eye, axis=0, keepdims=True) + EPS)
            rk = lax.rsqrt(jnp.sum(k32 * k32, axis=1, keepdims=True) + EPS)
            rq = lax.rsqrt(jnp.sum(q32 * q32, axis=1, keepdims=True) + EPS) * (D**-0.5)
            kkn = kk * rk * rk_row
            qkn = qk * rq * rk_row
            g_rows = scal[kh, :, c * C : (c + 1) * C]
            cols = g_rows.T
            for e in range(2):
                g_row = g_rows[e : e + 1, :]
                g = cols[:, e : e + 1]
                b = cols[:, 2 + e : 3 + e]
                ratio = jnp.exp(jnp.where(row >= col, g - g_row, NEG))
                low = jnp.where(row > col, ratio * kkn * b, 0.0)
                eg = jnp.exp(g)
                g_end = g[C - 1 : C, :]
                v32 = vf[pl.ds(c * C * HEADS + 2 * kh + e, C, stride=HEADS), :]
                cells.append(dict(
                    low=low, sc=split(ratio * qkn), egq=eg * rq, e_end=jnp.exp(g_end),
                    out=jnp.exp(g_end - g) * rk,
                    rhs=jnp.concatenate([b * v32, (b * eg * rk) * k32], axis=1),
                ))
            qs.append((q32, q16))
            kts.append(kt16)
        invs = [-jnp.where((row >> 1) == (col >> 1), x["low"], 0.0) for x in cells]
        for lg in range(1, 7):
            here = ((row >> (lg + 1)) == (col >> (lg + 1))) & ((row >> lg) != (col >> lg))
            offs = [jnp.where(here, x["low"], 0.0) for x in cells]
            i16 = [x.astype(BF16) for x in invs]
            ys = [o + dot(i, o.astype(BF16)) for o, i in zip(offs, i16)]
            zs = [dot(y.astype(BF16), i) for y, i in zip(ys, i16)]
            invs = [v - (y + z) for v, y, z in zip(invs, ys, zs)]
        xs = [x["rhs"] + dot(i.astype(BF16), x["rhs"].astype(BF16)) for x, i in zip(cells, invs)]
        rp, acc = [None, None], [None, None]
        for c in range(NCH):
            q32, q16 = qs[c]
            two = [cells[2 * c], cells[2 * c + 1]]
            xx = [xs[2 * c], xs[2 * c + 1]]
            if c == 0:
                uws = [jnp.concatenate([x[:, :D], -x[:, D:]], axis=1) for x in xx]
            else:
                rp16 = [r.astype(BF16) for r in rp]
                wrps = [dot(x[:, D:].astype(BF16), r) for x, r in zip(xx, rp16)]
                uws = [
                    jnp.concatenate([x[:, :D] - p[:, :D], -(a * x[:, D:] + p[:, D:])], axis=1)
                    for x, p, a in zip(xx, wrps, acc)
                ]
            sp = [split(x["out"] * u) for x, u in zip(two, uws)]
            kt2 = jnp.concatenate([kts[c], kts[c]], axis=1)
            adds = [dot(kt2, jnp.concatenate([h, l], axis=0)) for h, l in sp]
            ogs = []
            for e in range(2):
                u16 = uws[e].astype(BF16)
                ogs.append(dot(
                    jnp.concatenate(two[e]["sc"], axis=1), jnp.concatenate([u16, u16], axis=0)
                ))
            if c > 0:
                ogs = [o + x["egq"] * dot(q16, r) for o, x, r in zip(ogs, two, rp16)]
            for e in range(2):
                hd = 2 * kh + e
                x = two[e]
                direct = x["egq"] if c == 0 else x["egq"] * acc[e]
                o0[hd, c * C : (c + 1) * C, :] = ogs[e][:, :D]
                gh, gl = split(ogs[e][:, D:] + direct * q32)
                gq[hd, c * C : (c + 1) * C, :D] = gh
                gq[hd, c * C : (c + 1) * C, D:] = gl
                rp[e] = adds[e] if c == 0 else x["e_end"] * rp[e] + adds[e]
                acc[e] = x["e_end"] if c == 0 else x["e_end"] * acc[e]
        for e in range(2):
            hd = 2 * kh + e
            bh, bl = split(rp[e][:, :D])
            wire[hd, 0:C, 0:D] = rp[e][:, D:].astype(BF16)
            wire[hd, 0:C, D : 2 * D] = bh
            wire[hd, 0:C, 2 * D : 3 * D] = bl
            a = jnp.broadcast_to(acc[e], (16, 3 * D))
            a0 = a.astype(BF16).astype(F32)
            a1 = (a - a0).astype(BF16).astype(F32)
            a2 = a - a0 - a1
            lane = lax.broadcasted_iota(jnp.int32, (16, 3 * D), 1)
            wire[hd, C : C + 16, :] = jnp.where(
                lane < D, a0, jnp.where(lane < 2 * D, a1, a2)
            ).astype(BF16)

            @pl.when(hd == j)
            def _():
                maps[j] = wire[hd]

            @pl.when(hd != j)
            def _():
                map_copy(hd, j, zh * HALF + hd).start()
        return 0

    lax.fori_loop(0, KHEADS, head, 0)

    for s in range(HALF):
        @pl.when(s != j)
        def _():
            map_copy(0, s, w).wait_recv()

    first = jnp.where(zh == 0, 1.0, 0.0)
    ent[0] = jnp.concatenate([prior[...] * first, jnp.zeros((D, D), F32)], axis=1)
    mul[0] = jnp.ones((8, D), F32)

    def link(i, _):
        m16 = maps[i, 0:C, 0:D]
        add = maps[i, 0:C, D : 2 * D].astype(F32) + maps[i, 0:C, 2 * D : 3 * D].astype(F32)
        ar = maps[i, C : C + 16, :].astype(F32)
        a = (ar[0:8, 0:D] + ar[0:8, D : 2 * D]) + ar[0:8, 2 * D : 3 * D]
        x = ent[i]
        xh, xl = split(x[:, :D])
        mx = dot(m16, jnp.concatenate([xh, xl, x[:, D:].astype(BF16)], axis=1))
        acc = mul[i]
        a1 = a[0:1, :]
        r = a1 * x[:, :D] + (mx[:, :D] + mx[:, D : 2 * D]) + add
        p = a1 * x[:, D:] + mx[:, 2 * D :] + acc[0:1, :] * m16.astype(F32)
        ent[i + 1] = jnp.concatenate([r, p], axis=1)
        mul[i + 1] = a * acc
        return 0

    lax.fori_loop(0, HALF, link, 0)

    def z_copy(src, dst, i, to):
        return remote(src, dst, z_s.at[i], z_r.at[i], to)

    last = ent.at[HALF]
    to_one = [z_copy(last.at[:, pl.ds(0, D)], mid, 0, j + HALF)]
    to_zero = [
        z_copy(last, fin_z, 1, j),
        z_copy(mul.at[HALF], mul.at[HALF + 1], 2, j),
    ]

    def send_sin():
        for d in range(1, HALF):
            sin_copies[d - 1].start()

    sin_copies = [
        remote(
            sin16.at[(j + d) % HALF], sin.at[j], sin_s.at[d], sin_r.at[d],
            zh * HALF + (j + d) % HALF,
        )
        for d in range(1, HALF)
    ]
    fin_copies = [
        remote(finp, fin.at[j], fin_s.at[d], fin_r.at[d], zh * HALF + (j + d) % HALF)
        for d in range(1, HALF)
    ]

    @pl.when(zh == 0)
    def _():
        for copy in to_one:
            copy.start()

        def stage(i, _):
            sin16[i] = ent[i, :, 0:D].astype(BF16)
            return 0

        lax.fori_loop(0, HALF, stage, 0)
        send_sin()

    @pl.when(zh == 1)
    def _():
        for copy in to_zero:
            copy.start()

    for copy in att_copies:
        copy.wait()
    for i in range(4):
        own_k[2 * i : 2 * i + 2, :] = ak_ref[0, i].astype(F32)
    own = dot_nt(own_q[...], own_k[...].astype(BF16)) * (256**-0.5)
    r = lax.broadcasted_iota(jnp.int32, (16, 8), 0) // 4
    cc = lax.broadcasted_iota(jnp.int32, (16, 8), 1)
    own = jnp.where((cc % 2 == group) & (cc // 2 <= r), own, NEG)
    top = jnp.max(own, axis=1, keepdims=True)
    levels = []
    for s in range(WIDE):
        pk = parts[s, 16:32, :].astype(F32)
        lv = (pk[:, 0:1] + pk[:, 64:65]) + pk[:, 128:129]
        levels.append(lv)
        top = jnp.maximum(top, lv)
    pw = jnp.exp(own - top).astype(BF16)
    den = jnp.sum(pw.astype(F32), axis=1, keepdims=True)
    for i in range(4):
        own_k[2 * i : 2 * i + 2, :] = av_ref[0, i].astype(F32)
    num = dot(pw, own_k[...].astype(BF16))
    for s in range(WIDE):
        wt = jnp.exp(levels[s] - top)
        den = den + wt
        num = num + wt * parts[s, 0:16, :].astype(F32)
    for i in range(4):
        a0s[4 * i : 4 * i + 4, :] = ag_ref[0, i].astype(F32)
    done = num / den * sigmoid(a0s[...])
    for half in range(2):
        a1s[...] = done[:, half * 128 : (half + 1) * 128]
        for h in range(4):
            at = h * 256 + half * 128
            att_ref[0, :, at : at + 128] = a1s[pl.ds(h, 4, stride=4), :].astype(BF16)

    gain = gain_ref[...]
    vf[...] = gv[...].astype(F32)

    @pl.when(zh == 1)
    def _():
        to_one[0].wait_recv()
        s = mid[...]
        sh, sl = split(s)
        both = jnp.concatenate([sh, sl], axis=1)

        def enter(i, _):
            x = ent[i]
            y = dot(x[:, D:].astype(BF16), both)
            sin16[i] = (x[:, :D] + mul[i, 0:1, :] * s + (y[:, :D] + y[:, D:])).astype(BF16)
            return 0

        lax.fori_loop(0, HALF + 1, enter, 0)
        send_sin()
        finp[...] = sin16[HALF]

    @pl.when(zh == 0)
    def _():
        for copy in to_zero:
            copy.wait_recv()
        s = ent[HALF, :, 0:D]
        sh, sl = split(s)
        x = fin_z[...]
        y = dot(x[:, D:].astype(BF16), jnp.concatenate([sh, sl], axis=1))
        finp[...] = (
            x[:, :D] + mul[HALF + 1, 0:1, :] * s + (y[:, :D] + y[:, D:])
        ).astype(BF16)

    for copy in fin_copies:
        copy.start()
    fin[j] = finp[...]
    sin[j] = sin16[j]
    for copy in sin_copies:
        copy.wait()

    def finish(h, _):
        s = sin[h]
        o = o0[h] + dot(gq[h], jnp.concatenate([s, s], axis=0))
        scale = lax.rsqrt(jnp.mean(o * o, axis=1, keepdims=True) + EPS)
        z = vf[pl.ds(h, TOK, stride=HEADS), :]
        r = (o * scale * gain * (z * sigmoid(z))).astype(BF16)
        out_ref[:, pl.ds(pl.multiple_of(h * D, D), D)] = r
        return 0

    lax.fori_loop(0, HEADS, finish, 0)

    kraw, qraw = [], []
    for i in range(4):
        for ref, at, keep in ((sk_ref, 0, kraw), (sq_ref, 4, qraw)):
            x = ref[0, i].astype(F32)
            kqs[pl.ds(at + i, KHEADS, stride=8), :] = x
            uscr[pl.ds(0, KHEADS, stride=2), :] = x
            uscr[pl.ds(1, KHEADS, stride=2), :] = x
            keep.append(uscr[0:HEADS, :])
    rk = [lax.rsqrt(jnp.sum(x * x, axis=1, keepdims=True) + EPS) for x in kraw]
    rq = [lax.rsqrt(jnp.sum(x * x, axis=1, keepdims=True) + EPS) * (D**-0.5) for x in qraw]
    kn = [x * r for x, r in zip(kraw, rk)]
    qn = [x * r for x, r in zip(qraw, rq)]
    diag = lax.broadcasted_iota(jnp.int32, (HEADS, HEADS), 0) == lax.broadcasted_iota(
        jnp.int32, (HEADS, HEADS), 1
    )

    def column(x):
        return jnp.sum(jnp.where(diag, x, 0.0), axis=1, keepdims=True)

    sb = sigmoid(sb_ref[0])
    sd = sd_ref[0]
    beta = [column(sb[i : i + 1, :]) for i in range(4)]
    cum = [column(sd[0:1, :])]
    for i in range(1, 4):
        cum.append(cum[-1] + column(sd[i : i + 1, :]))
    for copy in fin_copies:
        copy.wait()
    for h in range(HEADS):
        kh = h // 2
        res[h * 8 : (h + 1) * 8, :] = dot(kqs[kh * 8 : (kh + 1) * 8, :].astype(BF16), fin[h])
    us = []
    for i in range(4):
        ks = res[pl.ds(i, HEADS, stride=8), :] * (rk[i] * jnp.exp(cum[i]))
        u = sv_ref[0, i].astype(F32) - ks
        for p in range(i):
            kk = jnp.sum(kn[i] * kn[p], axis=1, keepdims=True)
            u = u - (jnp.exp(cum[i] - cum[p]) * kk) * us[p]
        u = beta[i] * u
        us.append(u)
        o = res[pl.ds(4 + i, HEADS, stride=8), :] * (rq[i] * jnp.exp(cum[i]))
        for p in range(i + 1):
            qk = jnp.sum(qn[i] * kn[p], axis=1, keepdims=True)
            o = o + (jnp.exp(cum[i] - cum[p]) * qk) * us[p]
        scale = lax.rsqrt(jnp.mean(o * o, axis=1, keepdims=True) + EPS)
        z = sg_ref[0, i].astype(F32)
        sscr[i * 8 : (i + 1) * 8, :] = o * scale * gain * (z * sigmoid(z))
    for h in range(HEADS):
        step_ref[0, :, h * D : (h + 1) * D] = sscr[pl.ds(h, 4, stride=8), :].astype(BF16)
    for i in range(4):
        uscr[pl.ds(i, HEADS, stride=8), :] = us[i] * (jnp.exp(cum[3] - cum[i]) * rk[i])
        uscr[pl.ds(4 + i, HEADS, stride=8), :] = jnp.zeros((HEADS, D), F32)
    decay = jnp.broadcast_to(jnp.exp(cum[3]), (HEADS, D))
    for h in range(HEADS):
        kh = h // 2
        uh, ul = split(uscr[h * 8 : (h + 1) * 8, :])
        y = dot_tn(
            kqs[kh * 8 : (kh + 1) * 8, :].astype(BF16), jnp.concatenate([uh, ul], axis=1)
        )
        state_ref[0, h] = decay[h : h + 1, :] * fin[h].astype(F32) + (y[:, :D] + y[:, D:])

    for hd in range(HALF):
        @pl.when(hd != j)
        def _():
            map_copy(hd, 0, w).wait_send()

    @pl.when(zh == 0)
    def _():
        to_one[0].wait_send()

    @pl.when(zh == 1)
    def _():
        for copy in to_zero:
            copy.wait_send()


def shards(
    span_query, span_key, span_value, span_beta_logit, span_logdecay, span_gate,
    norm_gain, prior_state,
    step_query, step_key, step_value, step_beta_logit, step_logdecay, step_gate,
    cache_key, cache_value, att_query, att_key, att_value, att_gate,
):
    def rows(c):
        return c.reshape(2048, 2, 2, 128).transpose(0, 2, 1, 3).reshape(8192, 128)

    vm = pl.BlockSpec(memory_space=pltpu.VMEM)
    hbm = pl.BlockSpec(memory_space=pltpu.HBM)
    sem = pltpu.SemaphoreType.DMA
    V = pltpu.VMEM
    return pl.pallas_call(
        kernel,
        out_shape=(
            jax.ShapeDtypeStruct((TOK, HEADS * D), BF16),
            jax.ShapeDtypeStruct((1, 4, HEADS * D), BF16),
            jax.ShapeDtypeStruct((1, HEADS, D, D), F32),
            jax.ShapeDtypeStruct((1, 4, 1024), BF16),
        ),
        in_specs=[hbm, hbm, hbm, vm, vm, hbm, vm, hbm] + [vm] * 6 + [hbm, hbm] + [vm] * 4,
        out_specs=(vm,) * 4,
        scratch_shapes=[
            V((TOK * KHEADS, D), BF16), V((TOK * KHEADS, D), BF16), V((TOK * HEADS, D), BF16),
            V((TOK * HEADS, D), BF16), V((8192, D), BF16), V((8192, D), BF16), V((D, D), F32),
            V((TOK * KHEADS, D), F32), V((TOK * KHEADS, D), F32), V((TOK * HEADS, D), F32),
            V((8192, D), F32), V((2048, 256), BF16), V((2048, 256), BF16), V((256, 2048), F32),
            V((KHEADS, 8, TOK), F32),
            V((HEADS, C + 16, 3 * D), BF16), V((HALF, C + 16, 3 * D), BF16),
            V((HEADS, TOK, D), F32), V((HEADS, TOK, 2 * D), BF16),
            V((HALF + 1, D, 2 * D), F32), V((HALF + 2, 8, D), F32), V((D, D), F32),
            V((D, 2 * D), F32),
            V((HALF + 1, D, D), BF16), V((HALF, D, D), BF16), V((D, D), BF16),
            V((HALF, D, D), BF16),
            V((16, 256), BF16), V((WIDE, 16, 256), BF16),
            V((WIDE, 32, 256), BF16), V((WIDE, 32, 256), BF16),
            V((32, D), F32), V((64, D), F32), V((64, D), F32), V((32, D), F32),
            V((16, 256), F32), V((16, D), F32), V((8, 256), F32),
            sem((8,)), sem((WIDE,)), sem((WIDE,)), sem((WIDE,)), sem((WIDE,)),
            sem((HALF,)), sem((HALF,)), sem((HALF,)), sem((HALF,)), sem((HALF,)), sem((HALF,)),
            sem((3,)), sem((3,)),
        ],
        compiler_params=pltpu.CompilerParams(
            collective_id=0, has_side_effects=True, vmem_limit_bytes=56 * 2**20
        ),
        name="rollout_fork",
    )(
        span_query.reshape(TOK * KHEADS, D), span_key.reshape(TOK * KHEADS, D),
        span_value.reshape(TOK * HEADS, D), span_beta_logit.T, span_logdecay.T,
        span_gate.reshape(TOK * HEADS, D), norm_gain.reshape(1, D), prior_state,
        step_query, step_key, step_value, step_beta_logit, step_logdecay, step_gate,
        rows(cache_key), rows(cache_value), att_query, att_key, att_value, att_gate,
    )


def solution(mesh):
    tok = P(("prompt", "wide"), "tp", None)
    tok2 = P(("prompt", "wide"), "tp")
    stp = P(("prompt", "wide"), None, "tp", None)
    stp2 = P(("prompt", "wide"), None, "tp")
    in_specs = (
        tok, tok, tok, tok2, tok2, tok, P(), P(("prompt", "tp"), None, None),
        stp, stp, stp, stp2, stp2, stp,
        P(("prompt", "wide"), None, None), P(("prompt", "wide"), None, None),
        stp, P(("prompt", "wide"), None, None, None), P(("prompt", "wide"), None, None, None), stp,
    )
    out_specs = (
        P(("prompt", "wide"), "tp"),
        stp2,
        P(("prompt", "wide"), "tp", None, None),
        stp2,
    )
    return jax.shard_map(shards, mesh=mesh, in_specs=in_specs, out_specs=out_specs, check_vma=False)
```

time: 159 us -> 61.6 us (0.39)
  Pallas kernels: 108 us -> 56.5 us
  blocking collectives: 35.3 us -> 0 us
  local copies, waits for them, and re-layouts: 13.3 us -> 4.32 us
    pallas_call x4 -> x1, Pallas kernels: 108 us -> 56.5 us  [shards(): pl.pallas_call(kernel, out_shape=(jax.ShapeDtypeStruct((TOK, HEADS * D),...]
    all_gather x1 -> x0, blocking collectives: 35.3 us -> none  [shards(): lax.all_gather(att_query, 'wide', axis=0, tiled=True).reshape(256, 256)]
    dynamic_slice x1 -> x0, local copies, waits for them, and re-layouts: 5.72 us -> none  [shards(): lax.dynamic_index_in_dim(cache_value, group, axis=1, keepdims=False)]
    reshape x9 -> x0, local copies, waits for them, and re-layouts: 5.52 us -> none  [the longest x1 0.73 us: shards(): ldt = span_logdecay.T.reshape(KHEADS, 2, TOK)]
    unnamed x18 -> x10, local copies, waits for them, and re-layouts: 0.42 us -> 4.32 us
where the time goes in v2:
time: 61.6 us; the launch traced here: 61.5 us
  Pallas kernels  56.5 us (92%)
  local copies, waits for them, and re-layouts  4.32 us (7%)
  between operations  0.67 us (1%)
    pallas_call x1, Pallas kernels, shards(): pl.pallas_call(kernel, out_shape=(jax.ShapeDtypeStruct((TOK, HEADS * D),...  56.5 us
    unnamed x10, local copies, waits for them, and re-layouts  4.32 us

profile of v2, /device:TPU:1, one launch (start us, length us, event | category | flops | bytes accessed | tf_op | source)
XLA Modules:
  0.0 61.5 jit_solution(11549483436154374892)
XLA Ops:
  0.6 56.5 %rollout_fork.1 = (bf16[512,1024]{1,0:T(8,128)(2,1)}, bf16[1,4,1024]{2,1,0:T(4,128)(2,1)}, f32[1,8,128,128]{3,2,1,0:T(8,128)}, bf16[1,4,1024]{2,1,0:T(4,128)(2,1)}) custom-call(bf16[2048,128]{1,0:T(8,128)(2,1)} %bitcast.21, bf16[2048,128]{1,0:T(8,128)(2,1)} %bitcast.22, bf16[4096,128]{1,0:T(8,128)(2,1)} %bitcast.19, f32[8,512]{1,0:T(8,128)} %bitcast.23, ...), custom_call_target="tpu_custom_call" | custom-call | tf_op jit(solution)/shard_map/rollout_fork/pallas_call | solution.py:497
  57.1 0.0 copy-start.2
  57.1 0.0 copy-start
  57.1 0.0 copy-start.1
  57.1 2.3 %copy.30 = bf16[512,1024]{1,0:T(8,128)(2,1)} copy(bf16[512,1024]{1,0:T(8,128)(2,1)} %get-tuple-element.8) | data formatting | bytes 2097152
  59.5 0.0 copy-done.2
  59.5 0.6 copy.31
  60.1 0.0 copy-done
  60.1 0.8 %copy.32 = f32[1,8,128,128]{3,2,1,0:T(8,128)} copy(f32[1,8,128,128]{3,2,1,0:T(8,128)S(1)} %copy-done) | data formatting | bytes 1048576
  60.9 0.0 copy-done.1
  60.9 0.6 copy.33
Async XLA Ops:
  57.1 2.4 %copy-start.2 = (bf16[1,4,1024]{2,1,0:T(4,128)(2,1)S(1)}, bf16[1,4,1024]{2,1,0:T(4,128)(2,1)}, u32[]{:S(2)}) copy-start(bf16[1,4,1024]{2,1,0:T(4,128)(2,1)} %get-tuple-element.9) | copy-start | bytes 24580
  57.1 2.9 %copy-start = (f32[1,8,128,128]{3,2,1,0:T(8,128)S(1)}, f32[1,8,128,128]{3,2,1,0:T(8,128)}, u32[]{:S(2)}) copy-start(f32[1,8,128,128]{3,2,1,0:T(8,128)} %get-tuple-element.10) | copy-start | bytes 1572868
  57.1 3.7 %copy-start.1 = (bf16[1,4,1024]{2,1,0:T(4,128)(2,1)S(1)}, bf16[1,4,1024]{2,1,0:T(4,128)(2,1)}, u32[]{:S(2)}) copy-start(bf16[1,4,1024]{2,1,0:T(4,128)(2,1)} %get-tuple-element.11) | copy-start | bytes 24580

commit v3 on v2

--- a/solution.py
+++ b/solution.py
@@ -48,7 +48,7 @@
     out_ref, step_ref, state_ref, att_ref,
     qv, kv, vv, gv, ckv, cvv, prior,
     qf, kf, vf, cf, kc, vc, scores, scal,
-    wire, maps, o0, gq, ent, mul, mid, fin_z,
+    wire, maps, o0, gq, ent, mul, mid, fin_z, out_z,
     sin16, sin, finp, fin, own_q, all_q, msg, parts,
     kqs, res, uscr, sscr, a0s, a1s, own_k,
     load, q_s, q_r, att_s, att_r, map_s, map_r, sin_s, sin_r, fin_s, fin_r, z_s, z_r,
@@ -60,7 +60,7 @@
 
     loads = []
     for i, (src, dst) in enumerate((
-        (ck_hbm, ckv), (cv_hbm, cvv), (q_hbm, qv), (k_hbm, kv), (v_hbm, vv), (gate_hbm, gv),
+        (q_hbm, qv), (k_hbm, kv), (v_hbm, vv), (ck_hbm, ckv), (cv_hbm, cvv), (gate_hbm, gv),
         (prior_hbm.at[j], prior),
     )):
         copy = pltpu.make_async_copy(src, dst, load.at[i])
@@ -75,24 +75,6 @@
     for i in range(4):
         a0s[4 * i : 4 * i + 4, :] = aq_ref[0, i].astype(F32)
     own_q[...] = a0s[...].astype(BF16)
-    pl.semaphore_wait(barrier, WIDE - 1)
-
-    def remote(src, dst, ss, rs, to):
-        return pltpu.make_async_remote_copy(
-            src_ref=src, dst_ref=dst, send_sem=ss, recv_sem=rs,
-            device_id={"wide": to}, device_id_type=MESH,
-        )
-
-    def map_copy(to, slot, device):
-        return remote(wire.at[to], maps.at[slot], map_s.at[to], map_r.at[slot], device)
-
-    q_copies = []
-    for d in range(1, WIDE):
-        copy = remote(own_q, all_q.at[w], q_s.at[d], q_r.at[d], (w + d) % WIDE)
-        copy.start()
-        q_copies.append(copy)
-    all_q[w] = own_q[...]
-
     upper = (
         lax.broadcasted_iota(jnp.int32, (C, C), 0) <= lax.broadcasted_iota(jnp.int32, (C, C), 1)
     ).astype(F32)
@@ -108,41 +90,60 @@
             scal[kh, 0:2, part] = g8[2 * kh : 2 * kh + 2]
             scal[kh, 2:4, part] = b8[2 * kh : 2 * kh + 2]
 
-    for load_copy, raw, cut in ((loads[0], ckv, kc), (loads[1], cvv, vc)):
-        load_copy.wait()
-        cf[...] = raw[...].astype(F32)
-        cut[:, 0:128] = cf[pl.ds(group, 2048, stride=4), :].astype(BF16)
-        cut[:, 128:256] = cf[pl.ds(2 + group, 2048, stride=4), :].astype(BF16)
-    for copy in loads[2:]:
+    for copy in loads[:3]:
         copy.wait()
     qf[...] = qv[...].astype(F32)
     kf[...] = kv[...].astype(F32)
     vf[...] = vv[...].astype(F32)
-
-    for copy in q_copies:
-        copy.wait()
-    scores[...] = dot_nt(all_q[...].reshape(256, 256), kc[...]) * (256**-0.5)
-    sc = scores[...]
-    top = jnp.max(sc, axis=1, keepdims=True)
-    wt = jnp.exp(sc - top).astype(BF16)
-    total = jnp.sum(wt.astype(F32), axis=1, keepdims=True)
-    num = (dot(wt, vc[...]) / total).astype(BF16)
-    level = top + jnp.log(total)
-    l0 = level.astype(BF16).astype(F32)
-    l1 = (level - l0).astype(BF16).astype(F32)
-    l2 = level - l0 - l1
-    lane = lax.broadcasted_iota(jnp.int32, (256, 256), 1)
-    packed = jnp.where(lane < 64, l0, jnp.where(lane < 128, l1, l2)).astype(BF16)
-    for s in range(WIDE):
-        msg[s, 0:16, :] = num[s * 16 : (s + 1) * 16, :]
-        msg[s, 16:32, :] = packed[s * 16 : (s + 1) * 16, :]
+    pl.semaphore_wait(barrier, WIDE - 1)
+
+    def remote(src, dst, ss, rs, to):
+        return pltpu.make_async_remote_copy(
+            src_ref=src, dst_ref=dst, send_sem=ss, recv_sem=rs,
+            device_id={"wide": to}, device_id_type=MESH,
+        )
+
+    def map_copy(to, slot, device):
+        return remote(wire.at[to], maps.at[slot], map_s.at[to], map_r.at[slot], device)
+
+    q_copies = []
+    for d in range(1, WIDE):
+        copy = remote(own_q, all_q.at[w], q_s.at[d], q_r.at[d], (w + d) % WIDE)
+        copy.start()
+        q_copies.append(copy)
+    all_q[w] = own_q[...]
+
     att_copies = []
     for d in range(1, WIDE):
         to = (w + d) % WIDE
-        copy = remote(msg.at[to], parts.at[w], att_s.at[d], att_r.at[d], to)
-        copy.start()
-        att_copies.append(copy)
-    parts[w] = msg[w]
+        att_copies.append(remote(msg.at[to], parts.at[w], att_s.at[d], att_r.at[d], to))
+
+    def attend():
+        for load_copy, raw, cut in ((loads[3], ckv, kc), (loads[4], cvv, vc)):
+            load_copy.wait()
+            cf[...] = raw[...].astype(F32)
+            cut[:, 0:128] = cf[pl.ds(group, 2048, stride=4), :].astype(BF16)
+            cut[:, 128:256] = cf[pl.ds(2 + group, 2048, stride=4), :].astype(BF16)
+        for copy in q_copies:
+            copy.wait()
+        scores[...] = dot_nt(all_q[...].reshape(256, 256), kc[...]) * (256**-0.5)
+        sc = scores[...]
+        top = jnp.max(sc, axis=1, keepdims=True)
+        wt = jnp.exp(sc - top).astype(BF16)
+        total = jnp.sum(wt.astype(F32), axis=1, keepdims=True)
+        num = (dot(wt, vc[...]) / total).astype(BF16)
+        level = top + jnp.log(total)
+        l0 = level.astype(BF16).astype(F32)
+        l1 = (level - l0).astype(BF16).astype(F32)
+        l2 = level - l0 - l1
+        lane = lax.broadcasted_iota(jnp.int32, (256, 256), 1)
+        packed = jnp.where(lane < 64, l0, jnp.where(lane < 128, l1, l2)).astype(BF16)
+        for s in range(WIDE):
+            msg[s, 0:16, :] = num[s * 16 : (s + 1) * 16, :]
+            msg[s, 16:32, :] = packed[s * 16 : (s + 1) * 16, :]
+        for copy in att_copies:
+            copy.start()
+        parts[w] = msg[w]
 
     row = lax.broadcasted_iota(jnp.int32, (C, C), 0)
     col = lax.broadcasted_iota(jnp.int32, (C, C), 1)
@@ -150,6 +151,11 @@
     def head(it, _):
         kh = (j // 2 + jnp.where(it == 0, 2, 0) + jnp.where(it == 1, 1, 0)
               + jnp.where(it == 2, 3, 0)) % KHEADS
+
+        @pl.when(it == 1)
+        def _():
+            attend()
+
         ks, qs, kts, cells = [], [], [], []
         for c in range(NCH):
             k32 = kf[pl.ds(c * C * KHEADS + kh, C, stride=KHEADS), :]
@@ -192,41 +198,33 @@
             zs = [dot(y.astype(BF16), i) for y, i in zip(ys, i16)]
             invs = [v - (y + z) for v, y, z in zip(invs, ys, zs)]
         xs = [x["rhs"] + dot(i.astype(BF16), x["rhs"].astype(BF16)) for x, i in zip(cells, invs)]
-        rp, acc = [None, None], [None, None]
+        adds = []
         for c in range(NCH):
-            q32, q16 = qs[c]
-            two = [cells[2 * c], cells[2 * c + 1]]
-            xx = [xs[2 * c], xs[2 * c + 1]]
-            if c == 0:
-                uws = [jnp.concatenate([x[:, :D], -x[:, D:]], axis=1) for x in xx]
-            else:
-                rp16 = [r.astype(BF16) for r in rp]
-                wrps = [dot(x[:, D:].astype(BF16), r) for x, r in zip(xx, rp16)]
-                uws = [
-                    jnp.concatenate([x[:, :D] - p[:, :D], -(a * x[:, D:] + p[:, D:])], axis=1)
-                    for x, p, a in zip(xx, wrps, acc)
-                ]
-            sp = [split(x["out"] * u) for x, u in zip(two, uws)]
             kt2 = jnp.concatenate([kts[c], kts[c]], axis=1)
-            adds = [dot(kt2, jnp.concatenate([h, l], axis=0)) for h, l in sp]
-            ogs = []
             for e in range(2):
-                u16 = uws[e].astype(BF16)
-                ogs.append(dot(
-                    jnp.concatenate(two[e]["sc"], axis=1), jnp.concatenate([u16, u16], axis=0)
-                ))
-            if c > 0:
-                ogs = [o + x["egq"] * dot(q16, r) for o, x, r in zip(ogs, two, rp16)]
+                i = 2 * c + e
+                h, l = split(cells[i]["out"] * xs[i])
+                adds.append(dot(kt2, jnp.concatenate([h, l], axis=0)))
+        rps, accs = [[None, None]], [[None, None]]
+        for c in range(NCH):
+            nrp, nacc = [], []
             for e in range(2):
-                hd = 2 * kh + e
-                x = two[e]
-                direct = x["egq"] if c == 0 else x["egq"] * acc[e]
-                o0[hd, c * C : (c + 1) * C, :] = ogs[e][:, :D]
-                gh, gl = split(ogs[e][:, D:] + direct * q32)
-                gq[hd, c * C : (c + 1) * C, :D] = gh
-                gq[hd, c * C : (c + 1) * C, D:] = gl
-                rp[e] = adds[e] if c == 0 else x["e_end"] * rp[e] + adds[e]
-                acc[e] = x["e_end"] if c == 0 else x["e_end"] * acc[e]
+                i = 2 * c + e
+                e_end = cells[i]["e_end"]
+                inc, neg = adds[i][:, :D], -adds[i][:, D:]
+                if c == 0:
+                    nrp.append(jnp.concatenate([inc, neg], axis=1))
+                    nacc.append(e_end)
+                else:
+                    old, acc = rps[c][e], accs[c][e]
+                    nrp.append(
+                        e_end * old + jnp.concatenate([inc, acc * neg], axis=1)
+                        + dot(neg.astype(BF16), old.astype(BF16))
+                    )
+                    nacc.append(e_end * acc)
+            rps.append(nrp)
+            accs.append(nacc)
+        rp, acc = rps[NCH], accs[NCH]
         for e in range(2):
             hd = 2 * kh + e
             bh, bl = split(rp[e][:, :D])
@@ -249,9 +247,39 @@
             @pl.when(hd != j)
             def _():
                 map_copy(hd, j, zh * HALF + hd).start()
+        for c in range(NCH):
+            q32, q16 = qs[c]
+            for e in range(2):
+                hd = 2 * kh + e
+                x = xs[2 * c + e]
+                cell = cells[2 * c + e]
+                if c == 0:
+                    uw = jnp.concatenate([x[:, :D], -x[:, D:]], axis=1)
+                else:
+                    rp16 = rps[c][e].astype(BF16)
+                    p = dot(x[:, D:].astype(BF16), rp16)
+                    uw = jnp.concatenate(
+                        [x[:, :D] - p[:, :D], -(accs[c][e] * x[:, D:] + p[:, D:])], axis=1
+                    )
+                uh, ul = split(uw)
+                sch, scl = cell["sc"]
+                og = dot(
+                    jnp.concatenate([sch, scl, sch], axis=1),
+                    jnp.concatenate([uh, uh, ul], axis=0),
+                )
+                direct = cell["egq"]
+                if c > 0:
+                    og = og + direct * dot(q16, rp16)
+                    direct = direct * accs[c][e]
+                o0[hd, c * C : (c + 1) * C, :] = og[:, :D]
+                gh, gl = split(og[:, D:] + direct * q32)
+                gq[hd, c * C : (c + 1) * C, :D] = gh
+                gq[hd, c * C : (c + 1) * C, D:] = gl
         return 0
 
     lax.fori_loop(0, KHEADS, head, 0)
+    for copy in loads[5:]:
+        copy.wait()
 
     for s in range(HALF):
         @pl.when(s != j)
@@ -283,10 +311,10 @@
     def z_copy(src, dst, i, to):
         return remote(src, dst, z_s.at[i], z_r.at[i], to)
 
-    last = ent.at[HALF]
-    to_one = [z_copy(last.at[:, pl.ds(0, D)], mid, 0, j + HALF)]
+    out_z[...] = ent[HALF].astype(BF16)
+    to_one = [z_copy(out_z.at[:, pl.ds(0, D)], mid, 0, j + HALF)]
     to_zero = [
-        z_copy(last, fin_z, 1, j),
+        z_copy(out_z, fin_z, 1, j),
         z_copy(mul.at[HALF], mul.at[HALF + 1], 2, j),
     ]
 
@@ -362,19 +390,20 @@
     @pl.when(zh == 1)
     def _():
         to_one[0].wait_recv()
-        s = mid[...]
-        sh, sl = split(s)
-        both = jnp.concatenate([sh, sl], axis=1)
-
-        def enter(i, _):
+        s16 = mid[...]
+        s32 = s16.astype(F32)
+
+        def enter(i):
             x = ent[i]
-            y = dot(x[:, D:].astype(BF16), both)
-            sin16[i] = (x[:, :D] + mul[i, 0:1, :] * s + (y[:, :D] + y[:, D:])).astype(BF16)
-            return 0
-
-        lax.fori_loop(0, HALF + 1, enter, 0)
-        send_sin()
-        finp[...] = sin16[HALF]
+            y = dot(x[:, D:].astype(BF16), s16)
+            return (x[:, :D] + mul[i, 0:1, :] * s32 + y).astype(BF16)
+
+        for d in range(1, HALF):
+            to = (j + d) % HALF
+            sin16[to] = enter(to)
+            sin_copies[d - 1].start()
+        finp[...] = enter(HALF)
+        sin16[j] = enter(j)
 
     @pl.when(zh == 0)
     def _():
@@ -383,9 +412,9 @@
         s = ent[HALF, :, 0:D]
         sh, sl = split(s)
         x = fin_z[...]
-        y = dot(x[:, D:].astype(BF16), jnp.concatenate([sh, sl], axis=1))
+        y = dot(x[:, D:], jnp.concatenate([sh, sl], axis=1))
         finp[...] = (
-            x[:, :D] + mul[HALF + 1, 0:1, :] * s + (y[:, :D] + y[:, D:])
+            x[:, :D].astype(F32) + mul[HALF + 1, 0:1, :] * s + (y[:, :D] + y[:, D:])
         ).astype(BF16)
 
     for copy in fin_copies:
@@ -481,6 +510,11 @@
             copy.wait_send()
 
 
+def hand_out(a, b, c, d, ao, bo, co, do):
+    for src, dst in ((a, ao), (b, bo), (c, co), (d, do)):
+        dst[...] = src[...]
+
+
 def shards(
     span_query, span_key, span_value, span_beta_logit, span_logdecay, span_gate,
     norm_gain, prior_state,
@@ -494,7 +528,7 @@
     hbm = pl.BlockSpec(memory_space=pltpu.HBM)
     sem = pltpu.SemaphoreType.DMA
     V = pltpu.VMEM
-    return pl.pallas_call(
+    results = pl.pallas_call(
         kernel,
         out_shape=(
             jax.ShapeDtypeStruct((TOK, HEADS * D), BF16),
@@ -512,8 +546,8 @@
             V((KHEADS, 8, TOK), F32),
             V((HEADS, C + 16, 3 * D), BF16), V((HALF, C + 16, 3 * D), BF16),
             V((HEADS, TOK, D), F32), V((HEADS, TOK, 2 * D), BF16),
-            V((HALF + 1, D, 2 * D), F32), V((HALF + 2, 8, D), F32), V((D, D), F32),
-            V((D, 2 * D), F32),
+            V((HALF + 1, D, 2 * D), F32), V((HALF + 2, 8, D), F32), V((D, D), BF16),
+            V((D, 2 * D), BF16), V((D, 2 * D), BF16),
             V((HALF + 1, D, D), BF16), V((HALF, D, D), BF16), V((D, D), BF16),
             V((HALF, D, D), BF16),
             V((16, 256), BF16), V((WIDE, 16, 256), BF16),
@@ -525,7 +559,7 @@
             sem((3,)), sem((3,)),
         ],
         compiler_params=pltpu.CompilerParams(
-            collective_id=0, has_side_effects=True, vmem_limit_bytes=56 * 2**20
+            collective_id=0, has_side_effects=True, vmem_limit_bytes=59 * 2**20
         ),
         name="rollout_fork",
     )(
@@ -535,6 +569,14 @@
         step_query, step_key, step_value, step_beta_logit, step_logdecay, step_gate,
         rows(cache_key), rows(cache_value), att_query, att_key, att_value, att_gate,
     )
+    return pl.pallas_call(
+        hand_out,
+        out_shape=tuple(jax.ShapeDtypeStruct(x.shape, x.dtype) for x in results),
+        in_specs=[vm] * 4,
+        out_specs=(vm,) * 4,
+        compiler_params=pltpu.CompilerParams(vmem_limit_bytes=8 * 2**20),
+        name="hand_out",
+    )(*results)
 
 
 def solution(mesh):

time: 61.6 us -> 55.2 us (0.90)
  Pallas kernels: 56.5 us -> 50.6 us
  local copies, waits for them, and re-layouts: 4.32 us -> 3.65 us
    pallas_call x1, Pallas kernels: 56.5 us -> 49.4 us  [shards(): pl.pallas_call(kernel, out_shape=(jax.ShapeDtypeStruct((TOK, HEADS * D),...]
    pallas_call x0 -> x1, Pallas kernels: none -> 1.24 us  [shards(): pl.pallas_call(hand_out, out_shape=tuple((jax.ShapeDtypeStruct(x.shape, x...]
    unnamed x10 -> x8, local copies, waits for them, and re-layouts: 4.32 us -> 3.65 us
where the time goes in v3:
time: 55.2 us; the launch traced here: 54.9 us
  Pallas kernels  50.6 us (92%)
  local copies, waits for them, and re-layouts  3.65 us (7%)
  between operations  0.66 us (1%)
    pallas_call x1, Pallas kernels, shards(): pl.pallas_call(kernel, out_shape=(jax.ShapeDtypeStruct((TOK, HEADS * D),...  49.4 us
    unnamed x8, local copies, waits for them, and re-layouts  3.65 us
    pallas_call x1, Pallas kernels, shards(): pl.pallas_call(hand_out, out_shape=tuple((jax.ShapeDtypeStruct(x.shape, x...  1.24 us

profile of v3, /device:TPU:1, one launch (start us, length us, event | category | flops | bytes accessed | tf_op | source)
XLA Modules:
  0.0 54.9 jit_solution(16017102740168643840)
XLA Ops:
  0.6 49.4 %rollout_fork.1 = (bf16[512,1024]{1,0:T(8,128)(2,1)}, bf16[1,4,1024]{2,1,0:T(4,128)(2,1)}, f32[1,8,128,128]{3,2,1,0:T(8,128)}, bf16[1,4,1024]{2,1,0:T(4,128)(2,1)}) custom-call(bf16[2048,128]{1,0:T(8,128)(2,1)} %bitcast.21, bf16[2048,128]{1,0:T(8,128)(2,1)} %bitcast.22, bf16[4096,128]{1,0:T(8,128)(2,1)} %bitcast.19, f32[8,512]{1,0:T(8,128)} %bitcast.23, ...), custom_call_target="tpu_custom_call" | custom-call | tf_op jit(solution)/shard_map/rollout_fork/pallas_call | solution.py:531
  50.0 0.0 copy-start
  50.0 1.2 %copy-done = bf16[512,1024]{1,0:T(8,128)(2,1)S(1)} copy-done((bf16[512,1024]{1,0:T(8,128)(2,1)S(1)}, bf16[512,1024]{1,0:T(8,128)(2,1)}, u32[]{:S(2)}) %copy-start) | copy-done | bytes 1048600
  51.3 0.0 copy-start.1
  51.3 1.0 %copy-done.1 = f32[1,8,128,128]{3,2,1,0:T(8,128)S(1)} copy-done((f32[1,8,128,128]{3,2,1,0:T(8,128)S(1)}, f32[1,8,128,128]{3,2,1,0:T(8,128)}, u32[]{:S(2)}) %copy-start.1) | copy-done | bytes 524312
  52.3 0.0 copy-start.2
  52.3 0.7 %copy-done.2 = bf16[1,4,1024]{2,1,0:T(4,128)(2,1)S(1)} copy-done((bf16[1,4,1024]{2,1,0:T(4,128)(2,1)S(1)}, bf16[1,4,1024]{2,1,0:T(4,128)(2,1)}, u32[]{:S(2)}) %copy-start.2) | copy-done | bytes 8216
  53.0 0.0 copy-start.3
  53.0 0.7 %copy-done.3 = bf16[1,4,1024]{2,1,0:T(4,128)(2,1)S(1)} copy-done((bf16[1,4,1024]{2,1,0:T(4,128)(2,1)S(1)}, bf16[1,4,1024]{2,1,0:T(4,128)(2,1)}, u32[]{:S(2)}) %copy-start.3) | copy-done | bytes 8216
  53.7 1.2 %hand_out.1 = (bf16[512,1024]{1,0:T(8,128)(2,1)}, bf16[1,4,1024]{2,1,0:T(4,128)(2,1)}, f32[1,8,128,128]{3,2,1,0:T(8,128)}, bf16[1,4,1024]{2,1,0:T(4,128)(2,1)}) custom-call(bf16[512,1024]{1,0:T(8,128)(2,1)S(1)} %copy-done, bf16[1,4,1024]{2,1,0:T(4,128)(2,1)S(1)} %copy-done.2, f32[1,8,128,128]{3,2,1,0:T(8,128)S(1)} %copy-done.1, bf16[1,4,1024]{2,1,0:T(4,128)(2,1)S(1)} %copy-done.3), custom_call_target="tpu_custom_call" | custom-call | tf_op jit(solution)/shard_map/hand_out/pallas_call | solution.py:572
Async XLA Ops:
  50.0 1.2 %copy-start = (bf16[512,1024]{1,0:T(8,128)(2,1)S(1)}, bf16[512,1024]{1,0:T(8,128)(2,1)}, u32[]{:S(2)}) copy-start(bf16[512,1024]{1,0:T(8,128)(2,1)} %get-tuple-element.8.a) | copy-start | bytes 3145732
  51.3 1.0 %copy-start.1 = (f32[1,8,128,128]{3,2,1,0:T(8,128)S(1)}, f32[1,8,128,128]{3,2,1,0:T(8,128)}, u32[]{:S(2)}) copy-start(f32[1,8,128,128]{3,2,1,0:T(8,128)} %get-tuple-element.10.c) | copy-start | bytes 1572868
  52.3 0.7 %copy-start.2 = (bf16[1,4,1024]{2,1,0:T(4,128)(2,1)S(1)}, bf16[1,4,1024]{2,1,0:T(4,128)(2,1)}, u32[]{:S(2)}) copy-start(bf16[1,4,1024]{2,1,0:T(4,128)(2,1)} %get-tuple-element.9.b) | copy-start | bytes 24580
  53.0 0.7 %copy-start.3 = (bf16[1,4,1024]{2,1,0:T(4,128)(2,1)S(1)}, bf16[1,4,1024]{2,1,0:T(4,128)(2,1)}, u32[]{:S(2)}) copy-start(bf16[1,4,1024]{2,1,0:T(4,128)(2,1)} %get-tuple-element.11.d) | copy-start | bytes 24580

commit v4 on v3

--- a/solution.py
+++ b/solution.py
@@ -387,6 +387,13 @@
     gain = gain_ref[...]
     vf[...] = gv[...].astype(F32)
 
+    def gates(h, _):
+        z = vf[pl.ds(h, TOK, stride=HEADS), :]
+        cf[pl.ds(pl.multiple_of(h * TOK, TOK), TOK), :] = z * sigmoid(z) * gain
+        return 0
+
+    lax.fori_loop(0, HEADS, gates, 0)
+
     @pl.when(zh == 1)
     def _():
         to_one[0].wait_recv()
@@ -421,19 +428,15 @@
         copy.start()
     fin[j] = finp[...]
     sin[j] = sin16[j]
-    for copy in sin_copies:
-        copy.wait()
-
-    def finish(h, _):
+    for d in range(HALF):
+        h = (j + HALF - d) % HALF
+        if d > 0:
+            sin_copies[d - 1].wait_recv()
         s = sin[h]
         o = o0[h] + dot(gq[h], jnp.concatenate([s, s], axis=0))
         scale = lax.rsqrt(jnp.mean(o * o, axis=1, keepdims=True) + EPS)
-        z = vf[pl.ds(h, TOK, stride=HEADS), :]
-        r = (o * scale * gain * (z * sigmoid(z))).astype(BF16)
-        out_ref[:, pl.ds(pl.multiple_of(h * D, D), D)] = r
-        return 0
-
-    lax.fori_loop(0, HEADS, finish, 0)
+        z = cf[pl.ds(pl.multiple_of(h * TOK, TOK), TOK), :]
+        out_ref[:, pl.ds(pl.multiple_of(h * D, D), D)] = (o * scale * z).astype(BF16)
 
     kraw, qraw = [], []
     for i in range(4):
@@ -500,6 +503,9 @@
         def _():
             map_copy(hd, 0, w).wait_send()
 
+    for copy in sin_copies:
+        copy.wait_send()
+
     @pl.when(zh == 0)
     def _():
         to_one[0].wait_send()
@@ -531,10 +537,10 @@
     results = pl.pallas_call(
         kernel,
         out_shape=(
-            jax.ShapeDtypeStruct((TOK, HEADS * D), BF16),
-            jax.ShapeDtypeStruct((1, 4, HEADS * D), BF16),
-            jax.ShapeDtypeStruct((1, HEADS, D, D), F32),
-            jax.ShapeDtypeStruct((1, 4, 1024), BF16),
+            V((TOK, HEADS * D), BF16),
+            V((1, 4, HEADS * D), BF16),
+            V((1, HEADS, D, D), F32),
+            V((1, 4, 1024), BF16),
         ),
         in_specs=[hbm, hbm, hbm, vm, vm, hbm, vm, hbm] + [vm] * 6 + [hbm, hbm] + [vm] * 4,
         out_specs=(vm,) * 4,
@@ -559,7 +565,7 @@
             sem((3,)), sem((3,)),
         ],
         compiler_params=pltpu.CompilerParams(
-            collective_id=0, has_side_effects=True, vmem_limit_bytes=59 * 2**20
+            collective_id=0, has_side_effects=True, vmem_limit_bytes=58 * 2**20
         ),
         name="rollout_fork",
     )(

time: 55.2 us -> 50.2 us (0.909)
  local copies, waits for them, and re-layouts: 3.65 us -> 0 us
  Pallas kernels: 50.6 us -> 49.5 us
    unnamed x8 -> x0, local copies, waits for them, and re-layouts: 3.65 us -> none
    pallas_call x1, Pallas kernels: 49.4 us -> 48.2 us  [shards(): pl.pallas_call(kernel, out_shape=(V((TOK, HEADS * D), BF16), V((1, 4, HEA...]
where the time goes in v4:
time: 50.2 us; the launch traced here: 50.1 us
  Pallas kernels  49.5 us (99%)
  between operations  0.65 us (1%)
    pallas_call x1, Pallas kernels, shards(): pl.pallas_call(kernel, out_shape=(V((TOK, HEADS * D), BF16), V((1, 4, HEA...  48.2 us
    pallas_call x1, Pallas kernels, shards(): pl.pallas_call(hand_out, out_shape=tuple((jax.ShapeDtypeStruct(x.shape, x...  1.25 us

profile of v4, /device:TPU:1, one launch (start us, length us, event | category | flops | bytes accessed | tf_op | source)
XLA Modules:
  0.0 50.1 jit_solution(16163283801205162861)
XLA Ops:
  0.6 48.2 %rollout_fork.1 = (bf16[512,1024]{1,0:T(8,128)(2,1)S(1)}, bf16[1,4,1024]{2,1,0:T(4,128)(2,1)S(1)}, f32[1,8,128,128]{3,2,1,0:T(8,128)S(1)}, bf16[1,4,1024]{2,1,0:T(4,128)(2,1)S(1)}) custom-call(bf16[2048,128]{1,0:T(8,128)(2,1)} %bitcast.21, bf16[2048,128]{1,0:T(8,128)(2,1)} %bitcast.22, bf16[4096,128]{1,0:T(8,128)(2,1)} %bitcast.19, f32[8,512]{1,0:T(8,128)} %bitcast.23, ...), custom_call_target="tpu_custom_call" | custom-call | tf_op jit(solution)/shard_map/rollout_fork/pallas_call | solution.py:537
  48.9 1.2 %hand_out.1 = (bf16[512,1024]{1,0:T(8,128)(2,1)}, bf16[1,4,1024]{2,1,0:T(4,128)(2,1)}, f32[1,8,128,128]{3,2,1,0:T(8,128)}, bf16[1,4,1024]{2,1,0:T(4,128)(2,1)}) custom-call(bf16[512,1024]{1,0:T(8,128)(2,1)S(1)} %get-tuple-element.8.a, bf16[1,4,1024]{2,1,0:T(4,128)(2,1)S(1)} %get-tuple-element.9.b, f32[1,8,128,128]{3,2,1,0:T(8,128)S(1)} %get-tuple-element.10.c, ...), custom_call_target="tpu_custom_call" | custom-call | tf_op jit(solution)/shard_map/hand_out/pallas_call | solution.py:578

commit v5 on v4

--- a/solution.py
+++ b/solution.py
@@ -152,7 +152,7 @@
         kh = (j // 2 + jnp.where(it == 0, 2, 0) + jnp.where(it == 1, 1, 0)
               + jnp.where(it == 2, 3, 0)) % KHEADS
 
-        @pl.when(it == 1)
+        @pl.when(it == 2)
         def _():
             attend()
 
@@ -163,7 +163,7 @@
             k16 = k32.astype(BF16)
             q16 = q32.astype(BF16)
             kt16 = k32.T.astype(BF16)
-            kq = dot(jnp.concatenate([k16, q16], axis=0), kt16)
+            kq = dot_nt(jnp.concatenate([k16, q16], axis=0), k16)
             kk, qk = kq[:C], kq[C:]
             eye = jnp.where(row == col, kk, 0.0)
             rk_row = lax.rsqrt(jnp.sum(eye, axis=0, keepdims=True) + EPS)
@@ -189,8 +189,13 @@
                 ))
             qs.append((q32, q16))
             kts.append(kt16)
-        invs = [-jnp.where((row >> 1) == (col >> 1), x["low"], 0.0) for x in cells]
-        for lg in range(1, 7):
+        near = (row >> 2) == (col >> 2)
+        lows = [jnp.where(near, x["low"], 0.0) for x in cells]
+        l16 = [x.astype(BF16) for x in lows]
+        sq = [dot(x, x) for x in l16]
+        cu = [dot(x.astype(BF16), y) for x, y in zip(sq, l16)]
+        invs = [x - y - z for x, y, z in zip(sq, lows, cu)]
+        for lg in range(2, 7):
             here = ((row >> (lg + 1)) == (col >> (lg + 1))) & ((row >> lg) != (col >> lg))
             offs = [jnp.where(here, x["low"], 0.0) for x in cells]
             i16 = [x.astype(BF16) for x in invs]
@@ -394,50 +399,6 @@
 
     lax.fori_loop(0, HEADS, gates, 0)
 
-    @pl.when(zh == 1)
-    def _():
-        to_one[0].wait_recv()
-        s16 = mid[...]
-        s32 = s16.astype(F32)
-
-        def enter(i):
-            x = ent[i]
-            y = dot(x[:, D:].astype(BF16), s16)
-            return (x[:, :D] + mul[i, 0:1, :] * s32 + y).astype(BF16)
-
-        for d in range(1, HALF):
-            to = (j + d) % HALF
-            sin16[to] = enter(to)
-            sin_copies[d - 1].start()
-        finp[...] = enter(HALF)
-        sin16[j] = enter(j)
-
-    @pl.when(zh == 0)
-    def _():
-        for copy in to_zero:
-            copy.wait_recv()
-        s = ent[HALF, :, 0:D]
-        sh, sl = split(s)
-        x = fin_z[...]
-        y = dot(x[:, D:], jnp.concatenate([sh, sl], axis=1))
-        finp[...] = (
-            x[:, :D].astype(F32) + mul[HALF + 1, 0:1, :] * s + (y[:, :D] + y[:, D:])
-        ).astype(BF16)
-
-    for copy in fin_copies:
-        copy.start()
-    fin[j] = finp[...]
-    sin[j] = sin16[j]
-    for d in range(HALF):
-        h = (j + HALF - d) % HALF
-        if d > 0:
-            sin_copies[d - 1].wait_recv()
-        s = sin[h]
-        o = o0[h] + dot(gq[h], jnp.concatenate([s, s], axis=0))
-        scale = lax.rsqrt(jnp.mean(o * o, axis=1, keepdims=True) + EPS)
-        z = cf[pl.ds(pl.multiple_of(h * TOK, TOK), TOK), :]
-        out_ref[:, pl.ds(pl.multiple_of(h * D, D), D)] = (o * scale * z).astype(BF16)
-
     kraw, qraw = [], []
     for i in range(4):
         for ref, at, keep in ((sk_ref, 0, kraw), (sq_ref, 4, qraw)):
@@ -463,6 +424,54 @@
     cum = [column(sd[0:1, :])]
     for i in range(1, 4):
         cum.append(cum[-1] + column(sd[i : i + 1, :]))
+
+    @pl.when(zh == 1)
+    def _():
+        to_one[0].wait_recv()
+        s16 = mid[...]
+        s32 = s16.astype(F32)
+
+        def enter(i):
+            x = ent[i]
+            y = dot(x[:, D:].astype(BF16), s16)
+            return (x[:, :D] + mul[i, 0:1, :] * s32 + y).astype(BF16)
+
+        for d in range(1, HALF):
+            to = (j + d) % HALF
+            sin16[to] = enter(to)
+            sin_copies[d - 1].start()
+        finp[...] = enter(HALF)
+        for copy in fin_copies:
+            copy.start()
+        sin16[j] = enter(j)
+
+    @pl.when(zh == 0)
+    def _():
+        for copy in to_zero:
+            copy.wait_recv()
+        s = ent[HALF, :, 0:D]
+        sh, sl = split(s)
+        x = fin_z[...]
+        y = dot(x[:, D:], jnp.concatenate([sh, sl], axis=1))
+        finp[...] = (
+            x[:, :D].astype(F32) + mul[HALF + 1, 0:1, :] * s + (y[:, :D] + y[:, D:])
+        ).astype(BF16)
+
+        for copy in fin_copies:
+            copy.start()
+
+    fin[j] = finp[...]
+    sin[j] = sin16[j]
+    for d in range(HALF):
+        h = (j + HALF - d) % HALF
+        if d > 0:
+            sin_copies[d - 1].wait_recv()
+        s = sin[h]
+        o = o0[h] + dot(gq[h], jnp.concatenate([s, s], axis=0))
+        scale = lax.rsqrt(jnp.mean(o * o, axis=1, keepdims=True) + EPS)
+        z = cf[pl.ds(pl.multiple_of(h * TOK, TOK), TOK), :]
+        out_ref[:, pl.ds(pl.multiple_of(h * D, D), D)] = (o * scale * z).astype(BF16)
+
     for copy in fin_copies:
         copy.wait()
     for h in range(HEADS):

time: 50.2 us -> 47.5 us (0.946)
  Pallas kernels: 49.5 us -> 46.7 us
    pallas_call x1, Pallas kernels: 48.2 us -> 45.4 us  [shards(): pl.pallas_call(kernel, out_shape=(V((TOK, HEADS * D), BF16), V((1, 4, HEA...]
where the time goes in v5:
time: 47.5 us; the launch traced here: 47.3 us
  Pallas kernels  46.7 us (98%)
  between operations  0.65 us (1%)
    pallas_call x1, Pallas kernels, shards(): pl.pallas_call(kernel, out_shape=(V((TOK, HEADS * D), BF16), V((1, 4, HEA...  45.4 us
    pallas_call x1, Pallas kernels, shards(): pl.pallas_call(hand_out, out_shape=tuple((jax.ShapeDtypeStruct(x.shape, x...  1.25 us

profile of v5, /device:TPU:1, one launch (start us, length us, event | category | flops | bytes accessed | tf_op | source)
XLA Modules:
  0.0 47.3 jit_solution(2978395210799063037)
XLA Ops:
  0.6 45.4 %rollout_fork.1 = (bf16[512,1024]{1,0:T(8,128)(2,1)S(1)}, bf16[1,4,1024]{2,1,0:T(4,128)(2,1)S(1)}, f32[1,8,128,128]{3,2,1,0:T(8,128)S(1)}, bf16[1,4,1024]{2,1,0:T(4,128)(2,1)S(1)}) custom-call(bf16[2048,128]{1,0:T(8,128)(2,1)} %bitcast.21, bf16[2048,128]{1,0:T(8,128)(2,1)} %bitcast.22, bf16[4096,128]{1,0:T(8,128)(2,1)} %bitcast.19, f32[8,512]{1,0:T(8,128)} %bitcast.23, ...), custom_call_target="tpu_custom_call" | custom-call | tf_op jit(solution)/shard_map/rollout_fork/pallas_call | solution.py:546
  46.1 1.2 %hand_out.1 = (bf16[512,1024]{1,0:T(8,128)(2,1)}, bf16[1,4,1024]{2,1,0:T(4,128)(2,1)}, f32[1,8,128,128]{3,2,1,0:T(8,128)}, bf16[1,4,1024]{2,1,0:T(4,128)(2,1)}) custom-call(bf16[512,1024]{1,0:T(8,128)(2,1)S(1)} %get-tuple-element.8.a, bf16[1,4,1024]{2,1,0:T(4,128)(2,1)S(1)} %get-tuple-element.9.b, f32[1,8,128,128]{3,2,1,0:T(8,128)S(1)} %get-tuple-element.10.c, ...), custom_call_target="tpu_custom_call" | custom-call | tf_op jit(solution)/shard_map/hand_out/pallas_call | solution.py:587
